TPU v7x, 512 devices: a whole 4x8x8 slice. The times are simulated.
512 devices in a mesh: replica: 32 (over z, x), tensor: 16 (over y, core).
Axes of the slice: x: 4, y: 8, z: 8, core: 2. Of those that a mesh axis runs over, the one named last changes fastest.
Arguments:
- queries: bfloat16 [1024, 8192], P('replica', 'tensor'), may hold values from -64 to 64
- cache_keys: bfloat16 [1024, 16, 128, 128], P('replica', 'tensor'), may hold values from -6 to 6
- cache_values: bfloat16 [1024, 16, 128, 128], P('replica', 'tensor'), may hold values from -6 to 6
- page_table: int32 [1024, 2], P('replica'), may hold values from 0 to 31, as said below
- live_slots: int32 [1024], P('replica'), may hold values from 1 to 256, 163840 in all
- migrations: int32 [256, 2], replicated, may hold values from 0 to 31, as said below
Outputs:
- attention: bfloat16 [1024, 8192], P('replica', 'tensor')
- moved_keys: bfloat16 [992, 16, 1, 128, 128], P('replica', 'tensor')
- moved_values: bfloat16 [992, 16, 1, 128, 128], P('replica', 'tensor')
Inputs may be any that keep to these rules, and one draw needn't show every extreme that they name: For each replica and each parity p, the entries of page_table at page positions of parity p name distinct pool pages of that replica. `migrations`: rows are grouped by source replica, 8 rows each, in the order of replicas. The sessions of one source are distinct; no destination is its source; at most 1 row of one source name the same destination, and some reach it; each replica is named by at most 31 rows, and some replica by exactly 31.
All inputs are finite; a program needn't handle non-finite values. No bound on the sum of `live_slots` on one device may be relied on, other than what follows from the above.
Results may differ from a plain program's by a relative error of at most 0.0085.
Values may be sent and summed in bfloat16 or wider, within the bound.
No kernel may reach another device: no remote copies, remote signals or barrier semaphores. Data moves between devices by JAX's collectives and lax.ppermute only.
A program may use at most 64 MiB of HBM per device.

v0:
```python
import math

import jax
import jax.numpy as jnp
from jax import lax
from jax.sharding import PartitionSpec as P

PPS = 2
CAP = 1
PH = 1


def partner(x, axis, bit):
    return lax.ppermute(x, axis, [(i, i ^ 1 << bit) for i in range(lax.axis_size(axis))])


def body(queries, cache_keys, cache_values, page_table, live_slots, migrations):
    replicas = lax.axis_size("replica")
    replica_id = lax.axis_index("replica")
    parity_bit = lax.axis_index("tensor") % 2
    head_dim = cache_keys.shape[3]
    page_len = cache_keys.shape[2]
    sessions = queries.shape[0]
    local_heads = queries.shape[1] // head_dim
    keys_pool = cache_keys[:, 0]
    values_pool = cache_values[:, 0]
    score_scale = 1.0 / math.sqrt(head_dim)
    table_pairs = page_table.reshape(sessions, PH, 2)
    own_pages = jnp.take(table_pairs, parity_bit, axis=2)
    own_queries = queries.reshape(sessions, local_heads, head_dim)
    partner_keys, partner_values = partner((cache_keys, cache_values), "tensor", 0)
    source_side = (jnp.arange(PPS, dtype=jnp.int32) % 2 != parity_bit).astype(jnp.int32)
    both_keys = jnp.stack([keys_pool, partner_keys[:, 0]])
    both_values = jnp.stack([values_pool, partner_values[:, 0]])
    full_keys = both_keys[source_side[None, :], page_table].reshape(
        sessions, PPS * page_len, head_dim
    )
    full_values = both_values[source_side[None, :], page_table].reshape(
        sessions, PPS * page_len, head_dim
    )
    slot_index = jnp.arange(PPS * page_len, dtype=jnp.int32)
    live_mask = slot_index[None, :] < live_slots[:, None]
    scores = (
        jnp.einsum("shd,scd->shc", own_queries, full_keys, preferred_element_type=jnp.float32)
        * score_scale
    )
    masked = jnp.where(live_mask[:, None, :], scores, -jnp.inf)
    peak = jnp.max(masked, axis=-1, keepdims=True)
    weights = jnp.exp(masked - peak)
    totals = jnp.sum(weights, axis=-1, keepdims=True)
    attended = jnp.einsum("shc,scd->shd", weights, full_values.astype(jnp.float32)) / totals
    attention = attended.reshape(sessions, local_heads * head_dim).astype(jnp.bfloat16)
    rows_all = migrations.shape[0]
    out_rows = rows_all // replicas
    in_most = replicas - 1
    row_ids = jnp.arange(rows_all, dtype=jnp.int32)
    sess_ids = migrations[:, 0]
    dest_ids = migrations[:, 1]
    source_ids = row_ids // out_rows
    earlier = row_ids[None, :] < row_ids[:, None]
    same_dest = dest_ids[None, :] == dest_ids[:, None]
    arrival = jnp.sum(earlier & same_dest, axis=1)
    pair_slot = jnp.sum(earlier & same_dest & (source_ids[None, :] == source_ids[:, None]), axis=1)
    my_sessions = lax.dynamic_slice_in_dim(sess_ids, replica_id * out_rows, out_rows)
    my_dests = lax.dynamic_slice_in_dim(dest_ids, replica_id * out_rows, out_rows)
    my_slots = lax.dynamic_slice_in_dim(pair_slot, replica_id * out_rows, out_rows)
    picked_pages = own_pages[my_sessions]
    payload = jnp.stack([keys_pool[picked_pages], values_pool[picked_pages]], axis=1).reshape(
        out_rows, -1
    )
    slot_count = replicas * CAP
    placing = (
        jnp.arange(slot_count, dtype=jnp.int32)[:, None] == (my_dests * CAP + my_slots)[None, :]
    ).astype(jnp.bfloat16)
    packed = jnp.dot(placing, payload, preferred_element_type=jnp.float32).astype(jnp.bfloat16)
    received = lax.all_to_all(packed, "replica", split_axis=0, concat_axis=0, tiled=True)
    arriving = dest_ids == replica_id
    choose_row = (
        (arrival[None, :] == jnp.arange(in_most, dtype=jnp.int32)[:, None]) & arriving[None, :]
    ).astype(jnp.float32)
    row_to_slot = (
        jnp.arange(slot_count, dtype=jnp.int32)[None, :] == (source_ids * CAP + pair_slot)[:, None]
    ).astype(jnp.float32)
    selector = jnp.dot(choose_row, row_to_slot).astype(jnp.bfloat16)
    landed = jnp.dot(selector, received, preferred_element_type=jnp.float32).astype(jnp.bfloat16)
    landed = landed.reshape(in_most, 2, PH, page_len, head_dim)
    moved_keys = landed[:, 0:1]
    moved_values = landed[:, 1:2]
    return (attention, moved_keys, moved_values)


def solution(mesh):
    placed = (
        P("replica", "tensor"),
        P("replica", "tensor", None, None),
        P("replica", "tensor", None, None),
        P("replica", None),
        P("replica"),
        P(),
    )
    return jax.shard_map(
        body,
        mesh=mesh,
        in_specs=placed,
        out_specs=(
            P("replica", "tensor"),
            P("replica", "tensor", None, None, None),
            P("replica", "tensor", None, None, None),
        ),
        check_vma=False,
    )
```

profile of v0, /device:TPU:56, one launch (start us, length us, event | category | flops | bytes accessed | tf_op | source)
XLA Modules:
  0.0 92.9 jit_solution(10612735647225130335)
XLA Ops:
  0.7 0.8 fusion.32
  1.4 0.1 fusion.29
  1.5 0.7 fusion.25
  2.2 0.6 gather_fusion.2
  2.9 1.8 %gather_fusion.4 = bf16[8,128,128]{2,1,0:T(8,128)(2,1)S(1)} fusion(bf16[32,128,128]{2,1,0:T(8,128)(2,1)} %bitcast.63, s32[1024]{0:T(1024)S(1)} %pad_clamp_fusion), kind=kCustom, calls=%fused_computation.4 | custom fusion | bytes 524320 | tf_op jit(solution)/shard_map/gather | solution.py:68
  4.7 1.8 %gather_fusion.3 = bf16[8,128,128]{2,1,0:T(8,128)(2,1)S(1)} fusion(bf16[32,128,128]{2,1,0:T(8,128)(2,1)} %bitcast.66, s32[1024]{0:T(1024)S(1)} %pad_clamp_fusion), kind=kCustom, calls=%fused_computation.3 | custom fusion | bytes 524320 | tf_op jit(solution)/shard_map/gather | solution.py:68
  6.5 0.1 pad_maximum_fusion.2
  6.6 0.2 reshape.143
  6.9 0.3 convert_reduce_fusion.1
  7.1 0.1 fusion.24
  7.2 0.7 fusion
  7.9 0.5 broadcast.275
  8.4 2.9 %reduce = bf16[32,32768]{1,0:T(8,128)(2,1)} reduce(bf16[32,1,32768]{2,0,1:T(8,128)(2,1)S(1)} %fusion, bf16[]{:T(256)} %broadcast.275), dimensions={1}, to_apply=%copy.38.reduce_sub_computation | reduce | bytes 4194306 | tf_op jit(solution)/shard_map/all_to_all | solution.py:76
  11.3 4.5 %reshape.232 = bf16[32,2,16384]{2,1,0:T(2,128)(2,1)} reshape(bf16[32,32768]{1,0:T(8,128)(2,1)} %reduce) | data formatting | bytes 4194304
  15.8 0.0 copy-start.1
  15.8 0.0 copy-start.4
  15.8 0.0 copy-start.3
  15.8 0.0 copy-start.5
  15.8 13.3 %all-to-all-start = ((bf16[32,2,16384]{2,1,0:T(2,128)(2,1)}), bf16[32,2,16384]{2,1,0:T(2,128)(2,1)S(1)}, u32[]{:S(2)}, u32[]{:S(2)}) async-start(bf16[32,2,16384]{2,1,0:T(2,128)(2,1)} %reshape.232), calls=%async_computation | async-start | bytes 4194304 | tf_op jit(solution)/shard_map/all_to_all | solution.py:76
  29.1 0.0 copy-done.1
  29.1 1.9 %collective-permute-start.1 = (bf16[32,1,128,128]{3,2,0,1:T(8,128)(2,1)S(1)}, bf16[32,1,128,128]{3,2,0,1:T(8,128)(2,1)}, u32[]{:S(2)}, u32[]{:S(2)}) collective-permute-start(bf16[32,1,128,128]{3,2,0,1:T(8,128)(2,1)S(1)} %bitcast.64), channel_id=1, source_target_pairs={{0,1},{1,0},{2,3},{3,2},{4,5},{5,4},{6,7},{7,6},{8,9},{9,8},{10,11... | collective-permute-start | bytes 3145736 | tf_op jit(solution)/shard_map/ppermute | solution.py:14
  31.1 2.4 %collective-permute-start = (bf16[32,1,128,128]{3,2,0,1:T(8,128)(2,1)}, bf16[32,1,128,128]{3,2,0,1:T(8,128)(2,1)}, u32[]{:S(2)}, u32[]{:S(2)}) collective-permute-start(bf16[32,1,128,128]{3,2,0,1:T(8,128)(2,1)} %bitcast.67), channel_id=1, source_target_pairs={{0,1},{1,0},{2,3},{3,2},{4,5},{5,4},{6,7},{7,6},{8,9},{9,8},{10,11... | collective-permute-start | bytes 3145736 | tf_op jit(solution)/shard_map/ppermute | solution.py:14
  33.5 0.0 copy-done.4
  33.5 0.1 fusion.22
  33.6 0.1 copy.35
  33.7 0.1 reshape.184
  33.8 0.0 copy-done.3
  33.8 0.0 copy-done.5
  33.8 0.1 iota_compare_fusion.5
  33.9 0.0 collective-permute-done.1
  33.9 2.7 %pad_maximum_fusion.1 = bf16[2,32,128,128]{3,2,1,0:T(8,128)(2,1)} fusion(bf16[1,32,128,128]{3,2,1,0:T(8,128)(2,1)} %bitcast.8, bf16[1,32,128,128]{3,2,1,0:T(8,128)(2,1)S(1)} %bitcast.65), kind=kLoop, calls=%fused_computation.9 | loop fusion | flops 1048576 | bytes 4194304 | tf_op jit(solution)/shard_map/stack | solution.py:34
  36.7 0.0 copy-start.2
  36.7 3.8 %gather_fusion.1 = bf16[64,128,128]{2,1,0:T(8,128)(2,1)} fusion(bf16[2,32,128,128]{3,2,1,0:T(8,128)(2,1)} %pad_maximum_fusion.1, s32[64]{0:T(128)S(1)} %reshape.184), kind=kCustom, calls=%fused_computation.1 | custom fusion | bytes 4194816 | tf_op jit(solution)/shard_map/gather | solution.py:38
  40.5 0.0 collective-permute-done
  40.5 0.0 copy-done.2
  40.5 2.7 %pad_maximum_fusion = bf16[2,32,128,128]{3,2,1,0:T(8,128)(2,1)} fusion(bf16[1,32,128,128]{3,2,1,0:T(8,128)(2,1)} %bitcast.2, bf16[1,32,128,128]{3,2,1,0:T(8,128)(2,1)S(1)} %bitcast.68), kind=kLoop, calls=%fused_computation.8 | loop fusion | flops 1048576 | bytes 4194304 | tf_op jit(solution)/shard_map/stack | solution.py:33
  43.2 3.8 %gather_fusion = bf16[64,128,128]{2,1,0:T(8,128)(2,1)} fusion(bf16[2,32,128,128]{3,2,1,0:T(8,128)(2,1)} %pad_maximum_fusion, s32[64]{0:T(128)S(1)} %reshape.184), kind=kCustom, calls=%fused_computation | custom fusion | bytes 4194816 | tf_op jit(solution)/shard_map/gather | solution.py:35
  47.0 2.5 %fusion.33 = (f32[32,4]{1,0:T(8,128)S(1)}, f32[32,4,256]{2,1,0:T(4,128)S(1)}) fusion(bf16[32,256,128]{2,1,0:T(8,128)(2,1)} %bitcast.58, bf16[32,4,128]{2,1,0:T(4,128)(2,1)S(1)} %reshape.140, pred[32,256]{1,0:T(8,128)(4,1)S(1)} %iota_compare_fusion.5), kind=kOutput, calls=%fused_computation.67 | convolution fusion | flops 8486784 | bytes 2269696 | tf_op jit(solution)/shard_map/shd,scd->shc/dot_general | solution.py:44
  49.4 0.2 fusion.7
  49.7 0.0 copy-done
  49.7 0.4 fusion.5
  50.1 0.6 copy.49
  50.7 28.5 %all-to-all-done = bf16[32,2,16384]{2,1,0:T(2,128)(2,1)S(1)} async-done(((bf16[32,2,16384]{2,1,0:T(2,128)(2,1)}), bf16[32,2,16384]{2,1,0:T(2,128)(2,1)S(1)}, u32[]{:S(2)}, u32[]{:S(2)}) %all-to-all-start) | async-done | bytes 2097184 | tf_op jit(solution)/shard_map/all_to_all | solution.py:76
  79.3 6.8 %reshape.233 = bf16[32,1,32768]{2,1,0:T(2,128)(2,1)} reshape(bf16[32,2,16384]{2,1,0:T(2,128)(2,1)S(1)} %all-to-all-done) | data formatting | bytes 4194304
  86.1 4.7 %convolution_convert_fusion = bf16[31,32768]{1,0:T(8,128)(2,1)S(1)} fusion(bf16[32,1,32768]{2,1,0:T(2,128)(2,1)} %reshape.233, s32[256]{0:T(256)S(1)} %fusion.30, s32[256]{0:T(256)S(1)} %get-tuple-element.14, pred[256]{0:T(512)(128)(4,1)S(1)} %broadcast_compare_fusion), kind=kOutput, calls=%fused_computation.5 | convolution fusion | flops 66560480 | bytes 4131072 | tf_op jit(solution)/shard_map/dot_general | solution.py:85
  90.8 0.5 copy.43
  91.3 0.2 slice.37
  91.5 1.4 %fusion.31 = (bf16[31,1,1,128,128]{4,3,2,1,0:T(8,128)(2,1)}, bf16[31,1,1,128,128]{4,3,2,1,0:T(8,128)(2,1)}) fusion(bf16[31,2,1,128,128]{4,3,2,1,0:T(8,128)(2,1)S(1)} %bitcast.61), kind=kLoop, calls=%fused_computation.65 | loop fusion | bytes 4063232 | tf_op jit(solution)/shard_map/slice | solution.py:88
  (10 shorter events, 0.1 us)
Async XLA Ops:
  15.8 13.3 %copy-start.1 = (bf16[32,1,128,128]{3,2,1,0:T(8,128)(2,1)S(1)}, bf16[32,1,128,128]{3,2,1,0:T(8,128)(2,1)}, u32[]{:S(2)}) copy-start(bf16[32,1,128,128]{3,2,1,0:T(8,128)(2,1)} %param.8) | copy-start | bytes 3145732
  15.8 17.7 %copy-start.4 = (s32[32,2]{0,1:T(2,128)S(1)}, s32[32,2]{0,1:T(2,128)}, u32[]{:S(2)}) copy-start(s32[32,2]{0,1:T(2,128)} %param.9) | copy-start | bytes 772
  15.8 18.0 %copy-start.3 = (bf16[32,512]{1,0:T(8,128)(2,1)S(1)}, bf16[32,512]{1,0:T(8,128)(2,1)}, u32[]{:S(2)}) copy-start(bf16[32,512]{1,0:T(8,128)(2,1)} %param.6) | copy-start | bytes 98308
  15.8 18.0 %copy-start.5 = (s32[32]{0:T(128)S(1)}, s32[32]{0:T(128)}, u32[]{:S(2)}) copy-start(s32[32]{0:T(128)} %param.10) | copy-start | bytes 388
  15.8 63.5 %all-to-all-start = ((bf16[32,2,16384]{2,1,0:T(2,128)(2,1)}), bf16[32,2,16384]{2,1,0:T(2,128)(2,1)S(1)}, u32[]{:S(2)}, u32[]{:S(2)}) async-start(bf16[32,2,16384]{2,1,0:T(2,128)(2,1)} %reshape.232), calls=%async_computation | async-start | bytes 4194304 | tf_op jit(solution)/shard_map/all_to_all | solution.py:76
  29.1 4.8 %collective-permute-start.1 = (bf16[32,1,128,128]{3,2,0,1:T(8,128)(2,1)S(1)}, bf16[32,1,128,128]{3,2,0,1:T(8,128)(2,1)}, u32[]{:S(2)}, u32[]{:S(2)}) collective-permute-start(bf16[32,1,128,128]{3,2,0,1:T(8,128)(2,1)S(1)} %bitcast.64), channel_id=1, source_target_pairs={{0,1},{1,0},{2,3},{3,2},{4,5},{5,4},{6,7},{7,6},{8,9},{9,8},{10,11... | collective-permute-start | bytes 3145736 | tf_op jit(solution)/shard_map/ppermute | solution.py:14
  31.1 9.4 %collective-permute-start = (bf16[32,1,128,128]{3,2,0,1:T(8,128)(2,1)}, bf16[32,1,128,128]{3,2,0,1:T(8,128)(2,1)}, u32[]{:S(2)}, u32[]{:S(2)}) collective-permute-start(bf16[32,1,128,128]{3,2,0,1:T(8,128)(2,1)} %bitcast.67), channel_id=1, source_target_pairs={{0,1},{1,0},{2,3},{3,2},{4,5},{5,4},{6,7},{7,6},{8,9},{9,8},{10,11... | collective-permute-start | bytes 3145736 | tf_op jit(solution)/shard_map/ppermute | solution.py:14
  36.7 3.8 %copy-start.2 = (bf16[32,1,128,128]{3,2,1,0:T(8,128)(2,1)S(1)}, bf16[32,1,128,128]{3,2,1,0:T(8,128)(2,1)}, u32[]{:S(2)}) copy-start(bf16[32,1,128,128]{3,2,1,0:T(8,128)(2,1)} %param.7) | copy-start | bytes 3145732
  47.0 2.7 %copy-start = (bf16[64,128,128]{2,1,0:T(8,128)(2,1)S(1)}, bf16[64,128,128]{2,1,0:T(8,128)(2,1)}, u32[]{:S(2)}) copy-start(bf16[64,128,128]{2,1,0:T(8,128)(2,1)} %gather_fusion.1) | copy-start | bytes 6291460
where the time goes:
time: 93.5 us; the launch traced here: 92.9 us
  waiting for transfers between devices  28.5 us (30%)
  local copies, waits for them, and re-layouts  27.6 us (30%)
  starting transfers between devices  17.6 us (19%)
  other arithmetic  9.93 us (11%)
  matrix products  8.32 us (9%)
    all_to_all x1, waiting for transfers between devices, body(): lax.all_to_all(packed, 'replica', split_axis=0, concat_axis=0, tiled=True)  28.5 us
    all_to_all x1, starting transfers between devices, body(): lax.all_to_all(packed, 'replica', split_axis=0, concat_axis=0, tiled=True)  13.3 us
    unnamed x17, local copies, waits for them, and re-layouts  12.6 us
    dot_general x1, matrix products, body(): jnp.dot(selector, received, preferred_element_type=jnp.float32)  4.73 us
    ppermute x2, starting transfers between devices, partner(): lax.ppermute(x, axis, [(i, i ^ 1 << bit) for i in range(lax.axis_size(axi...  4.33 us
    gather x1, local copies, waits for them, and re-layouts, body(): both_values[source_side[None, :], page_table]  3.8 us
    gather x1, local copies, waits for them, and re-layouts, body(): both_keys[source_side[None, :], page_table]  3.76 us
    all_to_all x1, other arithmetic, body(): lax.all_to_all(packed, 'replica', split_axis=0, concat_axis=0, tiled=True)  2.91 us
  transfers between devices with their start and end apart: 3, of which 1 were waited for; matrix products, arithmetic and copies ran while one was open for 18% of the time, Pallas kernels for 0%

commit v1 on v0

v1 whole, which is shorter than its diff:
```python
import math

import jax
import jax.numpy as jnp
from jax import lax
from jax.experimental import pallas as pl
from jax.experimental.pallas import tpu as pltpu
from jax.sharding import PartitionSpec as P

OUT_ROWS = 8
ANY = pl.BlockSpec(memory_space=pl.ANY)
SMEM = pl.BlockSpec(memory_space=pltpu.SMEM)
VMEM = pl.BlockSpec(memory_space=pltpu.VMEM)


def partner(x, axis, bit):
    return lax.ppermute(x, axis, [(i, i ^ 1 << bit) for i in range(lax.axis_size(axis))])


def pack_kernel(table, moves, keys, values, packed, staged, in_sem, out_sem):
    replica, parity = lax.axis_index("replica"), lax.rem(lax.axis_index("tensor"), 2)
    page_len = keys.shape[2]
    loads, stores = [], []
    for j in range(OUT_ROWS):
        row = replica * OUT_ROWS + j
        page = table[parity, moves[0, row]]
        dest = moves[1, row]
        for half, pool in enumerate((keys, values)):
            part = staged.at[j, pl.ds(half * page_len, page_len)]
            loads.append(pltpu.make_async_copy(pool.at[page, 0], part, in_sem.at[2 * j + half]))
            loads[-1].start()
        stores.append(pltpu.make_async_copy(staged.at[j], packed.at[dest], out_sem.at[j]))
    for j, store in enumerate(stores):
        loads[2 * j].wait()
        loads[2 * j + 1].wait()
        store.start()
    for store in stores:
        store.wait()


def attention_kernel(
    table, live, moves, queries, own_k, own_v, other_k, other_v, out, order, qs, acc
):
    replica, parity = lax.axis_index("replica"), lax.rem(lax.axis_index("tensor"), 2)
    sessions, heads, head_dim = qs.shape
    page_len = own_k.shape[2]
    scale = 1.0 / math.sqrt(head_dim)

    def reset(a, carry):
        order[a] = -1
        return carry

    lax.fori_loop(0, order.shape[0], reset, 0)

    def arrive(m, count):
        here = moves[1, m] == replica

        @pl.when(here)
        def _():
            order[count] = m // OUT_ROWS

        return count + here.astype(jnp.int32)

    lax.fori_loop(0, moves.shape[1], arrive, jnp.int32(0))

    for h in range(heads):
        qs[:, h, :] = queries[:, h * head_dim : (h + 1) * head_dim].astype(jnp.float32)
    lane = lax.broadcasted_iota(jnp.int32, (heads, page_len), 1)
    contract_last = (((1,), (1,)), ((), ()))
    contract = (((1,), (0,)), ((), ()))

    def session(s):
        q = qs[s].astype(jnp.bfloat16)
        mine, theirs = table[parity, s], table[1 - parity, s]
        slots = live[s]
        s_own = lax.dot_general(
            q, own_k[mine, 0], contract_last, preferred_element_type=jnp.float32
        )
        s_oth = lax.dot_general(
            q, other_k[theirs, 0], contract_last, preferred_element_type=jnp.float32
        )
        s_own = jnp.where(lane < slots - parity * page_len, s_own * scale, -jnp.inf)
        s_oth = jnp.where(lane < slots - (1 - parity) * page_len, s_oth * scale, -jnp.inf)
        peak = jnp.maximum(
            jnp.max(s_own, axis=1, keepdims=True), jnp.max(s_oth, axis=1, keepdims=True)
        )
        w_own, w_oth = jnp.exp(s_own - peak), jnp.exp(s_oth - peak)
        total = jnp.sum(w_own, axis=1, keepdims=True) + jnp.sum(w_oth, axis=1, keepdims=True)
        o = lax.dot_general(
            w_own.astype(jnp.bfloat16), own_v[mine, 0], contract, preferred_element_type=jnp.float32
        ) + lax.dot_general(
            w_oth.astype(jnp.bfloat16),
            other_v[theirs, 0],
            contract,
            preferred_element_type=jnp.float32,
        )
        acc[s] = o / total

    def block(i, carry):
        for u in range(4):
            session(i * 4 + u)
        return carry

    lax.fori_loop(0, sessions // 4, block, 0)
    for h in range(heads):
        out[:, h * head_dim : (h + 1) * head_dim] = acc[:, h, :].astype(jnp.bfloat16)


def unpack_kernel(order, received, moved_k, moved_v, blank, sem):
    blank[...] = jnp.zeros_like(blank)
    page_len = blank.shape[0]
    slots = moved_k.shape[0]

    def place(a, carry):
        source = order[a]
        for half, moved in enumerate((moved_k, moved_v)):

            @pl.when(source >= 0)
            def _(half=half, moved=moved):
                pltpu.make_async_copy(
                    received.at[source, pl.ds(half * page_len, page_len)],
                    moved.at[a, 0, 0],
                    sem.at[half],
                ).start()

            @pl.when(source < 0)
            def _(half=half, moved=moved):
                pltpu.make_async_copy(blank, moved.at[a, 0, 0], sem.at[half]).start()

        return carry

    lax.fori_loop(0, slots, place, 0)
    for half, moved in enumerate((moved_k, moved_v)):
        pltpu.make_async_copy(moved, moved, sem.at[half]).wait()


def body(queries, cache_keys, cache_values, page_table, live_slots, migrations):
    replicas = lax.axis_size("replica")
    pool, _, page_len, head_dim = cache_keys.shape
    sessions = queries.shape[0]
    heads = queries.shape[1] // head_dim
    table, moves = page_table.T, migrations.T
    row = 2 * page_len
    packed = pl.pallas_call(
        pack_kernel,
        out_shape=jax.ShapeDtypeStruct((replicas, row, head_dim), jnp.bfloat16),
        in_specs=[SMEM, SMEM, ANY, ANY],
        out_specs=ANY,
        scratch_shapes=[
            pltpu.VMEM((OUT_ROWS, row, head_dim), jnp.bfloat16),
            pltpu.SemaphoreType.DMA((2 * OUT_ROWS,)),
            pltpu.SemaphoreType.DMA((OUT_ROWS,)),
        ],
        name="pack",
    )(table, moves, cache_keys, cache_values)
    received = lax.all_to_all(packed, "replica", split_axis=0, concat_axis=0, tiled=True)
    other_keys, other_values = partner((cache_keys, cache_values), "tensor", 0)
    attention, order = pl.pallas_call(
        attention_kernel,
        out_shape=(
            jax.ShapeDtypeStruct(queries.shape, jnp.bfloat16),
            jax.ShapeDtypeStruct((replicas,), jnp.int32),
        ),
        in_specs=[SMEM, SMEM, SMEM, VMEM, VMEM, VMEM, VMEM, VMEM],
        out_specs=(VMEM, SMEM),
        scratch_shapes=[
            pltpu.VMEM((sessions, heads, head_dim), jnp.float32),
            pltpu.VMEM((sessions, heads, head_dim), jnp.float32),
        ],
        compiler_params=pltpu.CompilerParams(vmem_limit_bytes=16 * 1024 * 1024),
        cost_estimate=pl.CostEstimate(
            flops=4 * sessions * heads * row * head_dim,
            bytes_accessed=8 * pool * page_len * head_dim,
            transcendentals=sessions * heads * row,
        ),
        name="attention",
    )(table, live_slots, moves, queries, cache_keys, cache_values, other_keys, other_values)
    moved = jax.ShapeDtypeStruct((replicas - 1, 1, 1, page_len, head_dim), jnp.bfloat16)
    moved_keys, moved_values = pl.pallas_call(
        unpack_kernel,
        out_shape=(moved, moved),
        in_specs=[SMEM, ANY],
        out_specs=(ANY, ANY),
        scratch_shapes=[
            pltpu.VMEM((page_len, head_dim), jnp.bfloat16),
            pltpu.SemaphoreType.DMA((2,)),
        ],
        compiler_params=pltpu.CompilerParams(vmem_limit_bytes=1024 * 1024),
        name="unpack",
    )(order, received)
    return attention, moved_keys, moved_values


def solution(mesh):
    placed = (
        P("replica", "tensor"),
        P("replica", "tensor", None, None),
        P("replica", "tensor", None, None),
        P("replica", None),
        P("replica"),
        P(),
    )
    return jax.shard_map(
        body,
        mesh=mesh,
        in_specs=placed,
        out_specs=(
            P("replica", "tensor"),
            P("replica", "tensor", None, None, None),
            P("replica", "tensor", None, None, None),
        ),
        check_vma=False,
    )
```

time: 93.5 us -> 69 us (0.74)
  local copies, waits for them, and re-layouts: 27.6 us -> 1.25 us
  Pallas kernels: 0 us -> 17.9 us
  other arithmetic: 9.93 us -> 0 us
  matrix products: 8.32 us -> 0 us
  waiting for transfers between devices: 28.5 us -> 31 us
    pallas_call x0 -> x3, Pallas kernels: none -> 17.9 us  [the longest x1 13.5 us: body(): pl.pallas_call(attention_kernel, out_shape=(jax.ShapeDtypeStruct(queries....]
    gather x5 -> x0, local copies, waits for them, and re-layouts: 11.8 us -> none  [the longest x1 3.8 us: body(): both_values[source_side[None, :], page_table]]
    unnamed x17 -> x12, local copies, waits for them, and re-layouts: 12.6 us -> 1.25 us
    dot_general x4 -> x0, matrix products: 8.32 us -> none  [the longest x1 4.73 us: body(): jnp.dot(selector, received, preferred_element_type=jnp.float32)]
    another operation x3 -> x0, other arithmetic: 5.55 us -> none  [the longest x1 2.75 us: body(): both_values = jnp.stack([values_pool, partner_values[:, 0]])]
    all_to_all x1 -> x0, other arithmetic: 2.91 us -> none  [body(): lax.all_to_all(packed, 'replica', split_axis=0, concat_axis=0, tiled=True)]
    ppermute x2, waiting for transfers between devices: 0.01 us -> 2.47 us  [partner(): lax.ppermute(x, axis, [(i, i ^ 1 << bit) for i in range(lax.axis_size(axi...]
    slice x2 -> x0, local copies, waits for them, and re-layouts: 2.19 us -> none  [the longest x1 1.43 us: body(): moved_values = landed[:, 1:2]]
  transfers between devices with their start and end apart: 3 -> 3, of which waited for: 1 -> 3; matrix products, arithmetic and copies ran while one was open for 18% -> 0% of each run, Pallas kernels for 0% -> 20%
where the time goes in v1:
time: 69 us; the launch traced here: 68.6 us
  waiting for transfers between devices  31 us (45%)
  Pallas kernels  17.9 us (26%)
  starting transfers between devices  17.6 us (26%)
  local copies, waits for them, and re-layouts  1.25 us (2%)
  between operations  0.73 us (1%)
    all_to_all x1, waiting for transfers between devices, body(): lax.all_to_all(packed, 'replica', split_axis=0, concat_axis=0, tiled=True)  28.5 us
    pallas_call x1, Pallas kernels, body(): pl.pallas_call(attention_kernel, out_shape=(jax.ShapeDtypeStruct(queries....  13.5 us
    all_to_all x1, starting transfers between devices, body(): lax.all_to_all(packed, 'replica', split_axis=0, concat_axis=0, tiled=True)  13.3 us
    ppermute x2, starting transfers between devices, partner(): lax.ppermute(x, axis, [(i, i ^ 1 << bit) for i in range(lax.axis_size(axi...  4.33 us
    pallas_call x1, Pallas kernels, body(): pl.pallas_call(pack_kernel, out_shape=jax.ShapeDtypeStruct((replicas, row...  2.57 us
    ppermute x2, waiting for transfers between devices, partner(): lax.ppermute(x, axis, [(i, i ^ 1 << bit) for i in range(lax.axis_size(axi...  2.47 us
    pallas_call x1, Pallas kernels, body(): pl.pallas_call(unpack_kernel, out_shape=(moved, moved), in_specs=[SMEM, A...  1.82 us
  transfers between devices with their start and end apart: 3, of which 3 were waited for; matrix products, arithmetic and copies ran while one was open for 0% of the time, Pallas kernels for 20%

profile of v1, /device:TPU:56, one launch (start us, length us, event | category | flops | bytes accessed | tf_op | source)
XLA Modules:
  0.0 68.6 jit_solution(11967272017132653283)
XLA Ops:
  0.6 2.6 %pack.1 = bf16[32,256,128]{2,1,0:T(8,128)(2,1)} custom-call(s32[2,32]{1,0:T(2,128)} %bitcast.4, s32[2,256]{1,0:T(2,128)} %bitcast.2, bf16[32,1,128,128]{3,2,1,0:T(8,128)(2,1)} %keys.1, bf16[32,1,128,128]{3,2,1,0:T(8,128)(2,1)} %values.1), custom_call_target="tpu_custom_call" | custom-call | tf_op jit(solution)/shard_map/pack/pallas_call | solution.py:144
  3.2 0.0 copy-start
  3.2 0.0 copy-start.2
  3.2 0.0 copy-start.3
  3.2 0.0 copy-start.4
  3.3 0.0 copy-start.5
  3.3 13.3 %all-to-all-start = ((bf16[32,256,128]{2,1,0:T(8,128)(2,1)}), bf16[32,256,128]{2,1,0:T(8,128)(2,1)S(1)}, u32[]{:S(2)}, u32[]{:S(2)}) async-start(bf16[32,256,128]{2,1,0:T(8,128)(2,1)} %pack.1), calls=%async_computation | async-start | bytes 4194304 | tf_op jit(solution)/shard_map/all_to_all | solution.py:156
  16.6 0.0 copy-done
  16.6 1.9 %collective-permute-start = (bf16[32,1,128,128]{3,2,1,0:T(8,128)(2,1)S(1)}, bf16[32,1,128,128]{3,2,1,0:T(8,128)(2,1)S(1)}, u32[]{:S(2)}, u32[]{:S(2)}) collective-permute-start(bf16[32,1,128,128]{3,2,1,0:T(8,128)(2,1)S(1)} %copy-done), channel_id=1, source_target_pairs={{0,1},{1,0},{2,3},{3,2},{4,5},{5,4},{6,7},{7,6},{8,9},{9,8},{10,11... | collective-permute-start | bytes 3145736 | tf_op jit(solution)/shard_map/ppermute | solution.py:17
  18.5 2.4 %collective-permute-start.1 = (bf16[32,1,128,128]{3,2,1,0:T(8,128)(2,1)}, bf16[32,1,128,128]{3,2,1,0:T(8,128)(2,1)S(1)}, u32[]{:S(2)}, u32[]{:S(2)}) collective-permute-start(bf16[32,1,128,128]{3,2,1,0:T(8,128)(2,1)} %values.1), channel_id=1, source_target_pairs={{0,1},{1,0},{2,3},{3,2},{4,5},{5,4},{6,7},{7,6},{8,9},{9,8},{10,11... | collective-permute-start | bytes 3145736 | tf_op jit(solution)/shard_map/ppermute | solution.py:17
  20.9 0.2 collective-permute-done.other_k
  21.1 2.3 %collective-permute-done.1.other_v = bf16[32,1,128,128]{3,2,1,0:T(8,128)(2,1)S(1)} collective-permute-done((bf16[32,1,128,128]{3,2,1,0:T(8,128)(2,1)}, bf16[32,1,128,128]{3,2,1,0:T(8,128)(2,1)S(1)}, u32[]{:S(2)}, u32[]{:S(2)}) %collective-permute-start.1) | collective-permute-done | bytes 1048608 | tf_op jit(solution)/shard_map/ppermute | solution.py:17
  23.4 0.0 copy-done.2
  23.4 0.0 copy-done.3
  23.4 0.0 copy-done.4
  23.4 0.0 copy-done.5
  23.4 0.0 copy-start.1
  23.4 1.2 %copy-done.1 = bf16[32,1,128,128]{3,2,1,0:T(8,128)(2,1)S(1)} copy-done((bf16[32,1,128,128]{3,2,1,0:T(8,128)(2,1)S(1)}, bf16[32,1,128,128]{3,2,1,0:T(8,128)(2,1)}, u32[]{:S(2)}) %copy-start.1) | copy-done | bytes 1048600
  24.7 13.5 %attention.1 = (bf16[32,512]{1,0:T(8,128)(2,1)}, s32[32]{0:T(128)S(1)}) custom-call(s32[2,32]{1,0:T(2,128)S(1)} %bitcast.5, s32[32]{0:T(128)S(1)} %copy-done.5, s32[2,256]{1,0:T(2,128)S(1)} %bitcast.3, bf16[32,512]{1,0:T(8,128)(2,1)S(1)} %copy-done.2, bf16[32,1,128,128]{3,2,1,0:T(8,128)(2,1)S(1)} %copy-done, bf16[32,1,128,128]{3,2,1,0:T(8,128)(2,1)S(1)} %copy-done.1, ...), custom_call_target="tpu_custom_call" | custom-call | flops 16777216 | bytes 4194304 | tf_op jit(solution)/shard_map/attention/pallas_call | solution.py:158
  38.2 28.5 %all-to-all-done.received = bf16[32,256,128]{2,1,0:T(8,128)(2,1)S(1)} async-done(((bf16[32,256,128]{2,1,0:T(8,128)(2,1)}), bf16[32,256,128]{2,1,0:T(8,128)(2,1)S(1)}, u32[]{:S(2)}, u32[]{:S(2)}) %all-to-all-start) | async-done | bytes 2097184 | tf_op jit(solution)/shard_map/all_to_all | solution.py:156
  66.7 1.8 %unpack.1 = (bf16[31,1,1,128,128]{4,3,2,1,0:T(8,128)(2,1)}, bf16[31,1,1,128,128]{4,3,2,1,0:T(8,128)(2,1)}) custom-call(s32[32]{0:T(128)S(1)} %get-tuple-element.8.order, bf16[32,256,128]{2,1,0:T(8,128)(2,1)S(1)} %all-to-all-done.received), custom_call_target="tpu_custom_call" | custom-call | tf_op jit(solution)/shard_map/unpack/pallas_call | solution.py:179
Async XLA Ops:
  3.2 13.4 %copy-start = (bf16[32,1,128,128]{3,2,1,0:T(8,128)(2,1)S(1)}, bf16[32,1,128,128]{3,2,1,0:T(8,128)(2,1)}, u32[]{:S(2)}) copy-start(bf16[32,1,128,128]{3,2,1,0:T(8,128)(2,1)} %keys.1) | copy-start | bytes 3145732
  3.2 20.2 %copy-start.2 = (bf16[32,512]{1,0:T(8,128)(2,1)S(1)}, bf16[32,512]{1,0:T(8,128)(2,1)}, u32[]{:S(2)}) copy-start(bf16[32,512]{1,0:T(8,128)(2,1)} %queries.1) | copy-start | bytes 98308
  3.2 20.2 %copy-start.3 = (s32[256,2]{0,1:T(2,128)S(1)}, s32[256,2]{0,1:T(2,128)}, u32[]{:S(2)}) copy-start(s32[256,2]{0,1:T(2,128)} %param.11) | copy-start | bytes 6148
  3.2 20.2 %copy-start.4 = (s32[32,2]{0,1:T(2,128)S(1)}, s32[32,2]{0,1:T(2,128)}, u32[]{:S(2)}) copy-start(s32[32,2]{0,1:T(2,128)} %param.9) | copy-start | bytes 772
  3.3 20.2 %copy-start.5 = (s32[32]{0:T(128)S(1)}, s32[32]{0:T(128)}, u32[]{:S(2)}) copy-start(s32[32]{0:T(128)} %live.1) | copy-start | bytes 388
  3.3 63.5 %all-to-all-start = ((bf16[32,256,128]{2,1,0:T(8,128)(2,1)}), bf16[32,256,128]{2,1,0:T(8,128)(2,1)S(1)}, u32[]{:S(2)}, u32[]{:S(2)}) async-start(bf16[32,256,128]{2,1,0:T(8,128)(2,1)} %pack.1), calls=%async_computation | async-start | bytes 4194304 | tf_op jit(solution)/shard_map/all_to_all | solution.py:156
  16.6 4.6 %collective-permute-start = (bf16[32,1,128,128]{3,2,1,0:T(8,128)(2,1)S(1)}, bf16[32,1,128,128]{3,2,1,0:T(8,128)(2,1)S(1)}, u32[]{:S(2)}, u32[]{:S(2)}) collective-permute-start(bf16[32,1,128,128]{3,2,1,0:T(8,128)(2,1)S(1)} %copy-done), channel_id=1, source_target_pairs={{0,1},{1,0},{2,3},{3,2},{4,5},{5,4},{6,7},{7,6},{8,9},{9,8},{10,11... | collective-permute-start | bytes 3145736 | tf_op jit(solution)/shard_map/ppermute | solution.py:17
  18.5 4.9 %collective-permute-start.1 = (bf16[32,1,128,128]{3,2,1,0:T(8,128)(2,1)}, bf16[32,1,128,128]{3,2,1,0:T(8,128)(2,1)S(1)}, u32[]{:S(2)}, u32[]{:S(2)}) collective-permute-start(bf16[32,1,128,128]{3,2,1,0:T(8,128)(2,1)} %values.1), channel_id=1, source_target_pairs={{0,1},{1,0},{2,3},{3,2},{4,5},{5,4},{6,7},{7,6},{8,9},{9,8},{10,11... | collective-permute-start | bytes 3145736 | tf_op jit(solution)/shard_map/ppermute | solution.py:17
  23.4 1.2 %copy-start.1 = (bf16[32,1,128,128]{3,2,1,0:T(8,128)(2,1)S(1)}, bf16[32,1,128,128]{3,2,1,0:T(8,128)(2,1)}, u32[]{:S(2)}) copy-start(bf16[32,1,128,128]{3,2,1,0:T(8,128)(2,1)} %values.1) | copy-start | bytes 3145732

commit v2 on v1

--- a/solution.py
+++ b/solution.py
@@ -8,6 +8,10 @@
 from jax.sharding import PartitionSpec as P
 
 OUT_ROWS = 8
+SEATS = (
+    28, 9, 19, 10, 29, 5, 7, 22, 0, 14, 8, 15, 23, 24, 21, 13,
+    25, 27, 6, 16, 26, 18, 11, 3, 17, 2, 1, 31, 12, 4, 30, 20,
+)
 ANY = pl.BlockSpec(memory_space=pl.ANY)
 SMEM = pl.BlockSpec(memory_space=pltpu.SMEM)
 VMEM = pl.BlockSpec(memory_space=pltpu.VMEM)
@@ -17,29 +21,44 @@
     return lax.ppermute(x, axis, [(i, i ^ 1 << bit) for i in range(lax.axis_size(axis))])
 
 
-def pack_kernel(table, moves, keys, values, packed, staged, in_sem, out_sem):
+def pack_kernel(
+    table_hbm, moves_hbm, seat_hbm, keys, values, packed,
+    table, moves, seat, pools, blank, in_sem, out_sem,
+):
     replica, parity = lax.axis_index("replica"), lax.rem(lax.axis_index("tensor"), 2)
     page_len = keys.shape[2]
-    loads, stores = [], []
+    loads = [
+        pltpu.make_async_copy(table_hbm, table, in_sem.at[0]),
+        pltpu.make_async_copy(moves_hbm, moves, in_sem.at[1]),
+        pltpu.make_async_copy(seat_hbm, seat, in_sem.at[2]),
+        pltpu.make_async_copy(keys.at[:, 0], pools.at[0], in_sem.at[3]),
+        pltpu.make_async_copy(values.at[:, 0], pools.at[1], in_sem.at[4]),
+    ]
+    for load in loads:
+        load.start()
+    blank[...] = jnp.zeros_like(blank)
+    for load in loads[:3]:
+        load.wait()
+    stores = [pltpu.make_async_copy(blank, packed.at[seat[replica]], out_sem.at[2 * OUT_ROWS])]
+    stores[0].start()
+    rows = []
     for j in range(OUT_ROWS):
         row = replica * OUT_ROWS + j
-        page = table[parity, moves[0, row]]
-        dest = moves[1, row]
-        for half, pool in enumerate((keys, values)):
-            part = staged.at[j, pl.ds(half * page_len, page_len)]
-            loads.append(pltpu.make_async_copy(pool.at[page, 0], part, in_sem.at[2 * j + half]))
-            loads[-1].start()
-        stores.append(pltpu.make_async_copy(staged.at[j], packed.at[dest], out_sem.at[j]))
-    for j, store in enumerate(stores):
-        loads[2 * j].wait()
-        loads[2 * j + 1].wait()
-        store.start()
+        rows.append((table[parity, moves[0, row]], seat[moves[1, row]]))
+    for half in range(2):
+        loads[3 + half].wait()
+        for j, (page, dest) in enumerate(rows):
+            slot = packed.at[dest, pl.ds(half * page_len, page_len)]
+            stores.append(
+                pltpu.make_async_copy(pools.at[half, page], slot, out_sem.at[2 * j + half])
+            )
+            stores[-1].start()
     for store in stores:
         store.wait()
 
 
 def attention_kernel(
-    table, live, moves, queries, own_k, own_v, other_k, other_v, out, order, qs, acc
+    table, live, moves, seat, queries, own_k, own_v, other_k, other_v, out, order, qs, acc
 ):
     replica, parity = lax.axis_index("replica"), lax.rem(lax.axis_index("tensor"), 2)
     sessions, heads, head_dim = qs.shape
@@ -47,7 +66,7 @@
     scale = 1.0 / math.sqrt(head_dim)
 
     def reset(a, carry):
-        order[a] = -1
+        order[a] = seat[replica]
         return carry
 
     lax.fori_loop(0, order.shape[0], reset, 0)
@@ -57,7 +76,7 @@
 
         @pl.when(here)
         def _():
-            order[count] = m // OUT_ROWS
+            order[count] = seat[m // OUT_ROWS]
 
         return count + here.astype(jnp.int32)
 
@@ -106,30 +125,13 @@
         out[:, h * head_dim : (h + 1) * head_dim] = acc[:, h, :].astype(jnp.bfloat16)
 
 
-def unpack_kernel(order, received, moved_k, moved_v, blank, sem):
-    blank[...] = jnp.zeros_like(blank)
-    page_len = blank.shape[0]
-    slots = moved_k.shape[0]
-
-    def place(a, carry):
+def unpack_kernel(order, received, moved_k, moved_v, sem):
+    page_len = moved_k.shape[3]
+    for a in range(moved_k.shape[0]):
         source = order[a]
         for half, moved in enumerate((moved_k, moved_v)):
-
-            @pl.when(source >= 0)
-            def _(half=half, moved=moved):
-                pltpu.make_async_copy(
-                    received.at[source, pl.ds(half * page_len, page_len)],
-                    moved.at[a, 0, 0],
-                    sem.at[half],
-                ).start()
-
-            @pl.when(source < 0)
-            def _(half=half, moved=moved):
-                pltpu.make_async_copy(blank, moved.at[a, 0, 0], sem.at[half]).start()
-
-        return carry
-
-    lax.fori_loop(0, slots, place, 0)
+            part = received.at[source, pl.ds(half * page_len, page_len)]
+            pltpu.make_async_copy(part, moved.at[a, 0, 0], sem.at[half]).start()
     for half, moved in enumerate((moved_k, moved_v)):
         pltpu.make_async_copy(moved, moved, sem.at[half]).wait()
 
@@ -140,20 +142,27 @@
     sessions = queries.shape[0]
     heads = queries.shape[1] // head_dim
     table, moves = page_table.T, migrations.T
+    seat = jnp.asarray([SEATS.index(r) for r in range(replicas)], jnp.int32)
     row = 2 * page_len
     packed = pl.pallas_call(
         pack_kernel,
         out_shape=jax.ShapeDtypeStruct((replicas, row, head_dim), jnp.bfloat16),
-        in_specs=[SMEM, SMEM, ANY, ANY],
+        in_specs=[ANY, ANY, ANY, ANY, ANY],
         out_specs=ANY,
         scratch_shapes=[
-            pltpu.VMEM((OUT_ROWS, row, head_dim), jnp.bfloat16),
-            pltpu.SemaphoreType.DMA((2 * OUT_ROWS,)),
-            pltpu.SemaphoreType.DMA((OUT_ROWS,)),
+            pltpu.SMEM(table.shape, jnp.int32),
+            pltpu.SMEM(moves.shape, jnp.int32),
+            pltpu.SMEM(seat.shape, jnp.int32),
+            pltpu.VMEM((2, pool, page_len, head_dim), jnp.bfloat16),
+            pltpu.VMEM((row, head_dim), jnp.bfloat16),
+            pltpu.SemaphoreType.DMA((5,)),
+            pltpu.SemaphoreType.DMA((2 * OUT_ROWS + 1,)),
         ],
         name="pack",
-    )(table, moves, cache_keys, cache_values)
-    received = lax.all_to_all(packed, "replica", split_axis=0, concat_axis=0, tiled=True)
+    )(table, moves, seat, cache_keys, cache_values)
+    received = lax.all_to_all(
+        packed, "replica", split_axis=0, concat_axis=0, axis_index_groups=[list(SEATS)], tiled=True
+    )
     other_keys, other_values = partner((cache_keys, cache_values), "tensor", 0)
     attention, order = pl.pallas_call(
         attention_kernel,
@@ -161,7 +170,7 @@
             jax.ShapeDtypeStruct(queries.shape, jnp.bfloat16),
             jax.ShapeDtypeStruct((replicas,), jnp.int32),
         ),
-        in_specs=[SMEM, SMEM, SMEM, VMEM, VMEM, VMEM, VMEM, VMEM],
+        in_specs=[SMEM, SMEM, SMEM, SMEM, VMEM, VMEM, VMEM, VMEM, VMEM],
         out_specs=(VMEM, SMEM),
         scratch_shapes=[
             pltpu.VMEM((sessions, heads, head_dim), jnp.float32),
@@ -174,17 +183,14 @@
             transcendentals=sessions * heads * row,
         ),
         name="attention",
-    )(table, live_slots, moves, queries, cache_keys, cache_values, other_keys, other_values)
+    )(table, live_slots, moves, seat, queries, cache_keys, cache_values, other_keys, other_values)
     moved = jax.ShapeDtypeStruct((replicas - 1, 1, 1, page_len, head_dim), jnp.bfloat16)
     moved_keys, moved_values = pl.pallas_call(
         unpack_kernel,
         out_shape=(moved, moved),
         in_specs=[SMEM, ANY],
         out_specs=(ANY, ANY),
-        scratch_shapes=[
-            pltpu.VMEM((page_len, head_dim), jnp.bfloat16),
-            pltpu.SemaphoreType.DMA((2,)),
-        ],
+        scratch_shapes=[pltpu.SemaphoreType.DMA((2,))],
         compiler_params=pltpu.CompilerParams(vmem_limit_bytes=1024 * 1024),
         name="unpack",
     )(order, received)

time: 69 us -> 66.6 us (0.965)
  waiting for transfers between devices: 31 us -> 28.1 us
    all_to_all x1, waiting for transfers between devices: 28.5 us -> 25.7 us  [body(): lax.all_to_all(packed, 'replica', split_axis=0, concat_axis=0, axis_index...]
  transfers between devices with their start and end apart: 3 -> 3, of which waited for: 3 -> 3; matrix products, arithmetic and copies ran while one was open for 0% -> 0% of each run, Pallas kernels for 20% -> 21%
where the time goes in v2:
time: 66.6 us; the launch traced here: 66.2 us
  waiting for transfers between devices  28.1 us (42%)
  Pallas kernels  18.1 us (27%)
  starting transfers between devices  18 us (27%)
  local copies, waits for them, and re-layouts  1.26 us (2%)
  between operations  0.75 us (1%)
    all_to_all x1, waiting for transfers between devices, body(): lax.all_to_all(packed, 'replica', split_axis=0, concat_axis=0, axis_index...  25.7 us
    pallas_call x1, Pallas kernels, body(): pl.pallas_call(attention_kernel, out_shape=(jax.ShapeDtypeStruct(queries....  13.8 us
    all_to_all x1, starting transfers between devices, body(): lax.all_to_all(packed, 'replica', split_axis=0, concat_axis=0, axis_index...  13.7 us
    ppermute x2, starting transfers between devices, partner(): lax.ppermute(x, axis, [(i, i ^ 1 << bit) for i in range(lax.axis_size(axi...  4.33 us
    ppermute x2, waiting for transfers between devices, partner(): lax.ppermute(x, axis, [(i, i ^ 1 << bit) for i in range(lax.axis_size(axi...  2.47 us
    pallas_call x1, Pallas kernels, body(): pl.pallas_call(pack_kernel, out_shape=jax.ShapeDtypeStruct((replicas, row...  2.45 us
    pallas_call x1, Pallas kernels, body(): pl.pallas_call(unpack_kernel, out_shape=(moved, moved), in_specs=[SMEM, A...  1.82 us
  transfers between devices with their start and end apart: 3, of which 3 were waited for; matrix products, arithmetic and copies ran while one was open for 0% of the time, Pallas kernels for 21%

profile of v2, /device:TPU:56, one launch (start us, length us, event | category | flops | bytes accessed | tf_op | source)
XLA Modules:
  0.0 66.2 jit_solution(7722538144139103217)
XLA Ops:
  0.6 2.5 %pack.1 = bf16[32,256,128]{2,1,0:T(8,128)(2,1)} custom-call(s32[2,32]{1,0:T(2,128)} %bitcast.4, s32[2,256]{1,0:T(2,128)} %bitcast.2, s32[32]{0:T(128)} %constant.2.clone.seat.seat_hbm, bf16[32,1,128,128]{3,2,1,0:T(8,128)(2,1)} %keys.1, bf16[32,1,128,128]{3,2,1,0:T(8,128)(2,1)} %values.1), custom_call_target="tpu_custom_call" | custom-call | tf_op jit(solution)/shard_map/pack/pallas_call | solution.py:147
  3.1 0.0 copy-start
  3.1 0.0 copy-start.2
  3.1 0.0 copy-start.3
  3.1 0.0 copy-start.4
  3.1 0.0 copy-start.5
  3.1 0.0 copy-start.6
  3.2 13.7 %all-to-all-start = ((bf16[32,256,128]{2,1,0:T(8,128)(2,1)}), bf16[32,256,128]{2,1,0:T(8,128)(2,1)S(1)}, u32[]{:S(2)}, u32[]{:S(2)}) async-start(bf16[32,256,128]{2,1,0:T(8,128)(2,1)} %pack.1), calls=%async_computation | async-start | bytes 4194304 | tf_op jit(solution)/shard_map/all_to_all | solution.py:163
  16.8 0.0 copy-done
  16.8 1.9 %collective-permute-start = (bf16[32,1,128,128]{3,2,1,0:T(8,128)(2,1)S(1)}, bf16[32,1,128,128]{3,2,1,0:T(8,128)(2,1)S(1)}, u32[]{:S(2)}, u32[]{:S(2)}) collective-permute-start(bf16[32,1,128,128]{3,2,1,0:T(8,128)(2,1)S(1)} %copy-done), channel_id=1, source_target_pairs={{0,1},{1,0},{2,3},{3,2},{4,5},{5,4},{6,7},{7,6},{8,9},{9,8},{10,11... | collective-permute-start | bytes 3145736 | tf_op jit(solution)/shard_map/ppermute | solution.py:21
  18.8 2.4 %collective-permute-start.1 = (bf16[32,1,128,128]{3,2,1,0:T(8,128)(2,1)}, bf16[32,1,128,128]{3,2,1,0:T(8,128)(2,1)S(1)}, u32[]{:S(2)}, u32[]{:S(2)}) collective-permute-start(bf16[32,1,128,128]{3,2,1,0:T(8,128)(2,1)} %values.1), channel_id=1, source_target_pairs={{0,1},{1,0},{2,3},{3,2},{4,5},{5,4},{6,7},{7,6},{8,9},{9,8},{10,11... | collective-permute-start | bytes 3145736 | tf_op jit(solution)/shard_map/ppermute | solution.py:21
  21.2 0.2 collective-permute-done.other_k
  21.4 2.3 %collective-permute-done.1.other_v = bf16[32,1,128,128]{3,2,1,0:T(8,128)(2,1)S(1)} collective-permute-done((bf16[32,1,128,128]{3,2,1,0:T(8,128)(2,1)}, bf16[32,1,128,128]{3,2,1,0:T(8,128)(2,1)S(1)}, u32[]{:S(2)}, u32[]{:S(2)}) %collective-permute-start.1) | collective-permute-done | bytes 1048608 | tf_op jit(solution)/shard_map/ppermute | solution.py:21
  23.7 0.0 copy-done.2
  23.7 0.0 copy-done.3
  23.7 0.0 copy-done.4
  23.7 0.0 copy-done.5
  23.7 0.0 copy-done.6
  23.7 0.0 copy-start.1
  23.7 1.2 %copy-done.1 = bf16[32,1,128,128]{3,2,1,0:T(8,128)(2,1)S(1)} copy-done((bf16[32,1,128,128]{3,2,1,0:T(8,128)(2,1)S(1)}, bf16[32,1,128,128]{3,2,1,0:T(8,128)(2,1)}, u32[]{:S(2)}) %copy-start.1) | copy-done | bytes 1048600
  24.9 13.8 %attention.1 = (bf16[32,512]{1,0:T(8,128)(2,1)}, s32[32]{0:T(128)S(1)}) custom-call(s32[2,32]{1,0:T(2,128)S(1)} %bitcast.5, s32[32]{0:T(128)S(1)} %copy-done.6, s32[2,256]{1,0:T(2,128)S(1)} %bitcast.3, s32[32]{0:T(128)S(1)} %copy-done.5, bf16[32,512]{1,0:T(8,128)(2,1)S(1)} %copy-done.2, bf16[32,1,128,128]{3,2,1,0:T(8,128)(2,1)S(1)} %copy-done, ...), custom_call_target="tpu_custom_call" | custom-call | flops 16777216 | bytes 4194304 | tf_op jit(solution)/shard_map/attention/pallas_call | solution.py:167
  38.7 25.7 %all-to-all-done.received = bf16[32,256,128]{2,1,0:T(8,128)(2,1)S(1)} async-done(((bf16[32,256,128]{2,1,0:T(8,128)(2,1)}), bf16[32,256,128]{2,1,0:T(8,128)(2,1)S(1)}, u32[]{:S(2)}, u32[]{:S(2)}) %all-to-all-start) | async-done | bytes 2097184 | tf_op jit(solution)/shard_map/all_to_all | solution.py:163
  64.4 1.8 %unpack.1 = (bf16[31,1,1,128,128]{4,3,2,1,0:T(8,128)(2,1)}, bf16[31,1,1,128,128]{4,3,2,1,0:T(8,128)(2,1)}) custom-call(s32[32]{0:T(128)S(1)} %get-tuple-element.8.order, bf16[32,256,128]{2,1,0:T(8,128)(2,1)S(1)} %all-to-all-done.received), custom_call_target="tpu_custom_call" | custom-call | tf_op jit(solution)/shard_map/unpack/pallas_call | solution.py:188
Async XLA Ops:
  3.1 13.7 %copy-start = (bf16[32,1,128,128]{3,2,1,0:T(8,128)(2,1)S(1)}, bf16[32,1,128,128]{3,2,1,0:T(8,128)(2,1)}, u32[]{:S(2)}) copy-start(bf16[32,1,128,128]{3,2,1,0:T(8,128)(2,1)} %keys.1) | copy-start | bytes 3145732
  3.1 20.6 %copy-start.2 = (bf16[32,512]{1,0:T(8,128)(2,1)S(1)}, bf16[32,512]{1,0:T(8,128)(2,1)}, u32[]{:S(2)}) copy-start(bf16[32,512]{1,0:T(8,128)(2,1)} %queries.1) | copy-start | bytes 98308
  3.1 20.6 %copy-start.3 = (s32[256,2]{0,1:T(2,128)S(1)}, s32[256,2]{0,1:T(2,128)}, u32[]{:S(2)}) copy-start(s32[256,2]{0,1:T(2,128)} %param.12) | copy-start | bytes 6148
  3.1 20.5 %copy-start.4 = (s32[32,2]{0,1:T(2,128)S(1)}, s32[32,2]{0,1:T(2,128)}, u32[]{:S(2)}) copy-start(s32[32,2]{0,1:T(2,128)} %param.10) | copy-start | bytes 772
  3.1 20.5 %copy-start.5 = (s32[32]{0:T(128)S(1)}, s32[32]{0:T(128)}, u32[]{:S(2)}) copy-start(s32[32]{0:T(128)} %constant.2.clone.seat.seat_hbm) | copy-start | bytes 388
  3.1 20.5 %copy-start.6 = (s32[32]{0:T(128)S(1)}, s32[32]{0:T(128)}, u32[]{:S(2)}) copy-start(s32[32]{0:T(128)} %live.1) | copy-start | bytes 388
  3.2 61.2 %all-to-all-start = ((bf16[32,256,128]{2,1,0:T(8,128)(2,1)}), bf16[32,256,128]{2,1,0:T(8,128)(2,1)S(1)}, u32[]{:S(2)}, u32[]{:S(2)}) async-start(bf16[32,256,128]{2,1,0:T(8,128)(2,1)} %pack.1), calls=%async_computation | async-start | bytes 4194304 | tf_op jit(solution)/shard_map/all_to_all | solution.py:163
  16.8 4.6 %collective-permute-start = (bf16[32,1,128,128]{3,2,1,0:T(8,128)(2,1)S(1)}, bf16[32,1,128,128]{3,2,1,0:T(8,128)(2,1)S(1)}, u32[]{:S(2)}, u32[]{:S(2)}) collective-permute-start(bf16[32,1,128,128]{3,2,1,0:T(8,128)(2,1)S(1)} %copy-done), channel_id=1, source_target_pairs={{0,1},{1,0},{2,3},{3,2},{4,5},{5,4},{6,7},{7,6},{8,9},{9,8},{10,11... | collective-permute-start | bytes 3145736 | tf_op jit(solution)/shard_map/ppermute | solution.py:21
  18.8 4.9 %collective-permute-start.1 = (bf16[32,1,128,128]{3,2,1,0:T(8,128)(2,1)}, bf16[32,1,128,128]{3,2,1,0:T(8,128)(2,1)S(1)}, u32[]{:S(2)}, u32[]{:S(2)}) collective-permute-start(bf16[32,1,128,128]{3,2,1,0:T(8,128)(2,1)} %values.1), channel_id=1, source_target_pairs={{0,1},{1,0},{2,3},{3,2},{4,5},{5,4},{6,7},{7,6},{8,9},{9,8},{10,11... | collective-permute-start | bytes 3145736 | tf_op jit(solution)/shard_map/ppermute | solution.py:21
  23.7 1.2 %copy-start.1 = (bf16[32,1,128,128]{3,2,1,0:T(8,128)(2,1)S(1)}, bf16[32,1,128,128]{3,2,1,0:T(8,128)(2,1)}, u32[]{:S(2)}) copy-start(bf16[32,1,128,128]{3,2,1,0:T(8,128)(2,1)} %values.1) | copy-start | bytes 3145732

commit v3 on v2

--- a/solution.py
+++ b/solution.py
@@ -9,8 +9,8 @@
 
 OUT_ROWS = 8
 SEATS = (
-    28, 9, 19, 10, 29, 5, 7, 22, 0, 14, 8, 15, 23, 24, 21, 13,
-    25, 27, 6, 16, 26, 18, 11, 3, 17, 2, 1, 31, 12, 4, 30, 20,
+    0, 21, 10, 15, 20, 25, 30, 3, 8, 13, 18, 23, 28, 1, 6, 11,
+    16, 5, 26, 31, 4, 9, 14, 19, 24, 29, 2, 7, 12, 17, 22, 27,
 )
 ANY = pl.BlockSpec(memory_space=pl.ANY)
 SMEM = pl.BlockSpec(memory_space=pltpu.SMEM)
@@ -39,12 +39,13 @@
     blank[...] = jnp.zeros_like(blank)
     for load in loads[:3]:
         load.wait()
-    stores = [pltpu.make_async_copy(blank, packed.at[seat[replica]], out_sem.at[2 * OUT_ROWS])]
+    own = packed.at[seat[parity, replica]]
+    stores = [pltpu.make_async_copy(blank, own, out_sem.at[2 * OUT_ROWS])]
     stores[0].start()
     rows = []
     for j in range(OUT_ROWS):
         row = replica * OUT_ROWS + j
-        rows.append((table[parity, moves[0, row]], seat[moves[1, row]]))
+        rows.append((table[parity, moves[0, row]], seat[parity, moves[1, row]]))
     for half in range(2):
         loads[3 + half].wait()
         for j, (page, dest) in enumerate(rows):
@@ -66,7 +67,7 @@
     scale = 1.0 / math.sqrt(head_dim)
 
     def reset(a, carry):
-        order[a] = seat[replica]
+        order[a] = seat[parity, replica]
         return carry
 
     lax.fori_loop(0, order.shape[0], reset, 0)
@@ -76,7 +77,7 @@
 
         @pl.when(here)
         def _():
-            order[count] = seat[m // OUT_ROWS]
+            order[count] = seat[parity, m // OUT_ROWS]
 
         return count + here.astype(jnp.int32)
 
@@ -142,7 +143,10 @@
     sessions = queries.shape[0]
     heads = queries.shape[1] // head_dim
     table, moves = page_table.T, migrations.T
-    seat = jnp.asarray([SEATS.index(r) for r in range(replicas)], jnp.int32)
+    orders = (SEATS, SEATS[::-1])
+    seat = jnp.asarray([[o.index(r) for r in range(replicas)] for o in orders], jnp.int32)
+    planes = lax.axis_size("tensor")
+    groups = [[r * planes + t for r in orders[t % 2]] for t in range(planes)]
     row = 2 * page_len
     packed = pl.pallas_call(
         pack_kernel,
@@ -161,7 +165,12 @@
         name="pack",
     )(table, moves, seat, cache_keys, cache_values)
     received = lax.all_to_all(
-        packed, "replica", split_axis=0, concat_axis=0, axis_index_groups=[list(SEATS)], tiled=True
+        packed,
+        ("replica", "tensor"),
+        split_axis=0,
+        concat_axis=0,
+        axis_index_groups=groups,
+        tiled=True,
     )
     other_keys, other_values = partner((cache_keys, cache_values), "tensor", 0)
     attention, order = pl.pallas_call(

time: 66.6 us -> 66.4 us (level)
  waiting for transfers between devices: 28.1 us -> 26.3 us
    all_to_all x1, waiting for transfers between devices: 25.7 us -> 23.5 us  [body(): lax.all_to_all(packed, ('replica', 'tensor'), split_axis=0, concat_axis=0...]
    ppermute x2, starting transfers between devices: 4.33 us -> 5.34 us  [partner(): lax.ppermute(x, axis, [(i, i ^ 1 << bit) for i in range(lax.axis_size(axi...]
  transfers between devices with their start and end apart: 3 -> 3, of which waited for: 3 -> 3; matrix products, arithmetic and copies ran while one was open for 0% -> 0% of each run, Pallas kernels for 21% -> 22%
where the time goes in v3:
time: 66.4 us; the launch traced here: 65.7 us
  waiting for transfers between devices  26.3 us (40%)
  Pallas kernels  18.7 us (28%)
  starting transfers between devices  18.6 us (28%)
  local copies, waits for them, and re-layouts  1.26 us (2%)
  between operations  0.75 us (1%)
    all_to_all x1, waiting for transfers between devices, body(): lax.all_to_all(packed, ('replica', 'tensor'), split_axis=0, concat_axis=0...  23.5 us
    pallas_call x1, Pallas kernels, body(): pl.pallas_call(attention_kernel, out_shape=(jax.ShapeDtypeStruct(queries....  14.4 us
    all_to_all x1, starting transfers between devices, body(): lax.all_to_all(packed, ('replica', 'tensor'), split_axis=0, concat_axis=0...  13.3 us
    ppermute x2, starting transfers between devices, partner(): lax.ppermute(x, axis, [(i, i ^ 1 << bit) for i in range(lax.axis_size(axi...  5.34 us
    ppermute x2, waiting for transfers between devices, partner(): lax.ppermute(x, axis, [(i, i ^ 1 << bit) for i in range(lax.axis_size(axi...  2.84 us
    pallas_call x1, Pallas kernels, body(): pl.pallas_call(pack_kernel, out_shape=jax.ShapeDtypeStruct((replicas, row...  2.46 us
    pallas_call x1, Pallas kernels, body(): pl.pallas_call(unpack_kernel, out_shape=(moved, moved), in_specs=[SMEM, A...  1.82 us
  transfers between devices with their start and end apart: 3, of which 3 were waited for; matrix products, arithmetic and copies ran while one was open for 0% of the time, Pallas kernels for 22%

profile of v3, /device:TPU:56, one launch (start us, length us, event | category | flops | bytes accessed | tf_op | source)
XLA Modules:
  0.0 65.7 jit_solution(2947210469060961010)
XLA Ops:
  0.6 2.5 %pack.1 = bf16[32,256,128]{2,1,0:T(8,128)(2,1)} custom-call(s32[2,32]{1,0:T(2,128)} %bitcast.4, s32[2,256]{1,0:T(2,128)} %bitcast.2, s32[2,32]{1,0:T(2,128)} %constant.2.clone.seat.seat_hbm, bf16[32,1,128,128]{3,2,1,0:T(8,128)(2,1)} %keys.1, bf16[32,1,128,128]{3,2,1,0:T(8,128)(2,1)} %values.1), custom_call_target="tpu_custom_call" | custom-call | tf_op jit(solution)/shard_map/pack/pallas_call | solution.py:151
  3.1 0.0 copy-start
  3.1 0.0 copy-start.2
  3.1 0.0 copy-start.3
  3.1 0.0 copy-start.4
  3.1 0.0 copy-start.5
  3.2 0.0 copy-start.6
  3.2 13.3 %all-to-all-start = ((bf16[32,256,128]{2,1,0:T(8,128)(2,1)}), bf16[32,256,128]{2,1,0:T(8,128)(2,1)S(1)}, u32[]{:S(2)}, u32[]{:S(2)}) async-start(bf16[32,256,128]{2,1,0:T(8,128)(2,1)} %pack.1), calls=%async_computation | async-start | bytes 4194304 | tf_op jit(solution)/shard_map/all_to_all | solution.py:167
  16.5 0.0 copy-done
  16.5 3.4 %collective-permute-start = (bf16[32,1,128,128]{3,2,1,0:T(8,128)(2,1)S(1)}, bf16[32,1,128,128]{3,2,1,0:T(8,128)(2,1)S(1)}, u32[]{:S(2)}, u32[]{:S(2)}) collective-permute-start(bf16[32,1,128,128]{3,2,1,0:T(8,128)(2,1)S(1)} %copy-done), channel_id=1, source_target_pairs={{0,1},{1,0},{2,3},{3,2},{4,5},{5,4},{6,7},{7,6},{8,9},{9,8},{10,11... | collective-permute-start | bytes 3145736 | tf_op jit(solution)/shard_map/ppermute | solution.py:21
  19.9 1.9 %collective-permute-start.1 = (bf16[32,1,128,128]{3,2,1,0:T(8,128)(2,1)}, bf16[32,1,128,128]{3,2,1,0:T(8,128)(2,1)S(1)}, u32[]{:S(2)}, u32[]{:S(2)}) collective-permute-start(bf16[32,1,128,128]{3,2,1,0:T(8,128)(2,1)} %values.1), channel_id=1, source_target_pairs={{0,1},{1,0},{2,3},{3,2},{4,5},{5,4},{6,7},{7,6},{8,9},{9,8},{10,11... | collective-permute-start | bytes 3145736 | tf_op jit(solution)/shard_map/ppermute | solution.py:21
  21.9 0.3 collective-permute-done.other_k
  22.2 2.5 %collective-permute-done.1.other_v = bf16[32,1,128,128]{3,2,1,0:T(8,128)(2,1)S(1)} collective-permute-done((bf16[32,1,128,128]{3,2,1,0:T(8,128)(2,1)}, bf16[32,1,128,128]{3,2,1,0:T(8,128)(2,1)S(1)}, u32[]{:S(2)}, u32[]{:S(2)}) %collective-permute-start.1) | collective-permute-done | bytes 1048608 | tf_op jit(solution)/shard_map/ppermute | solution.py:21
  24.7 0.0 copy-done.2
  24.7 0.0 copy-done.3
  24.7 0.0 copy-done.4
  24.7 0.0 copy-done.5
  24.7 0.0 copy-done.6
  24.7 0.0 copy-start.1
  24.7 1.2 %copy-done.1 = bf16[32,1,128,128]{3,2,1,0:T(8,128)(2,1)S(1)} copy-done((bf16[32,1,128,128]{3,2,1,0:T(8,128)(2,1)S(1)}, bf16[32,1,128,128]{3,2,1,0:T(8,128)(2,1)}, u32[]{:S(2)}) %copy-start.1) | copy-done | bytes 1048600
  26.0 14.4 %attention.1 = (bf16[32,512]{1,0:T(8,128)(2,1)}, s32[32]{0:T(128)S(1)}) custom-call(s32[2,32]{1,0:T(2,128)S(1)} %bitcast.5, s32[32]{0:T(128)S(1)} %copy-done.6, s32[2,256]{1,0:T(2,128)S(1)} %bitcast.3, s32[2,32]{1,0:T(2,128)S(1)} %copy-done.5, bf16[32,512]{1,0:T(8,128)(2,1)S(1)} %copy-done.2, bf16[32,1,128,128]{3,2,1,0:T(8,128)(2,1)S(1)} %copy-done, ...), custom_call_target="tpu_custom_call" | custom-call | flops 16777216 | bytes 4194304 | tf_op jit(solution)/shard_map/attention/pallas_call | solution.py:176
  40.3 23.5 %all-to-all-done.received = bf16[32,256,128]{2,1,0:T(8,128)(2,1)S(1)} async-done(((bf16[32,256,128]{2,1,0:T(8,128)(2,1)}), bf16[32,256,128]{2,1,0:T(8,128)(2,1)S(1)}, u32[]{:S(2)}, u32[]{:S(2)}) %all-to-all-start) | async-done | bytes 2097184 | tf_op jit(solution)/shard_map/all_to_all | solution.py:167
  63.8 1.8 %unpack.1 = (bf16[31,1,1,128,128]{4,3,2,1,0:T(8,128)(2,1)}, bf16[31,1,1,128,128]{4,3,2,1,0:T(8,128)(2,1)}) custom-call(s32[32]{0:T(128)S(1)} %get-tuple-element.8.order, bf16[32,256,128]{2,1,0:T(8,128)(2,1)S(1)} %all-to-all-done.received), custom_call_target="tpu_custom_call" | custom-call | tf_op jit(solution)/shard_map/unpack/pallas_call | solution.py:197
Async XLA Ops:
  3.1 13.4 %copy-start = (bf16[32,1,128,128]{3,2,1,0:T(8,128)(2,1)S(1)}, bf16[32,1,128,128]{3,2,1,0:T(8,128)(2,1)}, u32[]{:S(2)}) copy-start(bf16[32,1,128,128]{3,2,1,0:T(8,128)(2,1)} %keys.1) | copy-start | bytes 3145732
  3.1 21.6 %copy-start.2 = (bf16[32,512]{1,0:T(8,128)(2,1)S(1)}, bf16[32,512]{1,0:T(8,128)(2,1)}, u32[]{:S(2)}) copy-start(bf16[32,512]{1,0:T(8,128)(2,1)} %queries.1) | copy-start | bytes 98308
  3.1 21.6 %copy-start.3 = (s32[256,2]{0,1:T(2,128)S(1)}, s32[256,2]{0,1:T(2,128)}, u32[]{:S(2)}) copy-start(s32[256,2]{0,1:T(2,128)} %param.12) | copy-start | bytes 6148
  3.1 21.6 %copy-start.4 = (s32[32,2]{0,1:T(2,128)S(1)}, s32[32,2]{0,1:T(2,128)}, u32[]{:S(2)}) copy-start(s32[32,2]{0,1:T(2,128)} %param.10) | copy-start | bytes 772
  3.1 21.6 %copy-start.5 = (s32[2,32]{1,0:T(2,128)S(1)}, s32[2,32]{1,0:T(2,128)}, u32[]{:S(2)}) copy-start(s32[2,32]{1,0:T(2,128)} %constant.2.clone.seat.seat_hbm) | copy-start | bytes 772
  3.2 21.6 %copy-start.6 = (s32[32]{0:T(128)S(1)}, s32[32]{0:T(128)}, u32[]{:S(2)}) copy-start(s32[32]{0:T(128)} %live.1) | copy-start | bytes 388
  3.2 60.7 %all-to-all-start = ((bf16[32,256,128]{2,1,0:T(8,128)(2,1)}), bf16[32,256,128]{2,1,0:T(8,128)(2,1)S(1)}, u32[]{:S(2)}, u32[]{:S(2)}) async-start(bf16[32,256,128]{2,1,0:T(8,128)(2,1)} %pack.1), calls=%async_computation | async-start | bytes 4194304 | tf_op jit(solution)/shard_map/all_to_all | solution.py:167
  16.5 5.7 %collective-permute-start = (bf16[32,1,128,128]{3,2,1,0:T(8,128)(2,1)S(1)}, bf16[32,1,128,128]{3,2,1,0:T(8,128)(2,1)S(1)}, u32[]{:S(2)}, u32[]{:S(2)}) collective-permute-start(bf16[32,1,128,128]{3,2,1,0:T(8,128)(2,1)S(1)} %copy-done), channel_id=1, source_target_pairs={{0,1},{1,0},{2,3},{3,2},{4,5},{5,4},{6,7},{7,6},{8,9},{9,8},{10,11... | collective-permute-start | bytes 3145736 | tf_op jit(solution)/shard_map/ppermute | solution.py:21
  19.9 4.8 %collective-permute-start.1 = (bf16[32,1,128,128]{3,2,1,0:T(8,128)(2,1)}, bf16[32,1,128,128]{3,2,1,0:T(8,128)(2,1)S(1)}, u32[]{:S(2)}, u32[]{:S(2)}) collective-permute-start(bf16[32,1,128,128]{3,2,1,0:T(8,128)(2,1)} %values.1), channel_id=1, source_target_pairs={{0,1},{1,0},{2,3},{3,2},{4,5},{5,4},{6,7},{7,6},{8,9},{9,8},{10,11... | collective-permute-start | bytes 3145736 | tf_op jit(solution)/shard_map/ppermute | solution.py:21
  24.7 1.2 %copy-start.1 = (bf16[32,1,128,128]{3,2,1,0:T(8,128)(2,1)S(1)}, bf16[32,1,128,128]{3,2,1,0:T(8,128)(2,1)}, u32[]{:S(2)}) copy-start(bf16[32,1,128,128]{3,2,1,0:T(8,128)(2,1)} %values.1) | copy-start | bytes 3145732

commit v4 on v3

--- a/solution.py
+++ b/solution.py
@@ -58,12 +58,13 @@
         store.wait()
 
 
-def attention_kernel(
-    table, live, moves, seat, queries, own_k, own_v, other_k, other_v, out, order, qs, acc
+def partial_kernel(
+    table, live, moves, seat, queries, other_queries, keys, values, mine, theirs, order, qs
 ):
     replica, parity = lax.axis_index("replica"), lax.rem(lax.axis_index("tensor"), 2)
-    sessions, heads, head_dim = qs.shape
-    page_len = own_k.shape[2]
+    sessions, both, head_dim = qs.shape
+    heads = both // 2
+    page_len = keys.shape[2]
     scale = 1.0 / math.sqrt(head_dim)
 
     def reset(a, carry):
@@ -84,37 +85,33 @@
     lax.fori_loop(0, moves.shape[1], arrive, jnp.int32(0))
 
     for h in range(heads):
-        qs[:, h, :] = queries[:, h * head_dim : (h + 1) * head_dim].astype(jnp.float32)
-    lane = lax.broadcasted_iota(jnp.int32, (heads, page_len), 1)
-    contract_last = (((1,), (1,)), ((), ()))
-    contract = (((1,), (0,)), ((), ()))
+        part = slice(h * head_dim, (h + 1) * head_dim)
+        qs[:, h, :] = queries[:, part].astype(jnp.float32)
+        qs[:, heads + h, :] = other_queries[:, part].astype(jnp.float32)
+    lane = lax.broadcasted_iota(jnp.int32, (both, page_len), 1)
 
     def session(s):
-        q = qs[s].astype(jnp.bfloat16)
-        mine, theirs = table[parity, s], table[1 - parity, s]
-        slots = live[s]
-        s_own = lax.dot_general(
-            q, own_k[mine, 0], contract_last, preferred_element_type=jnp.float32
-        )
-        s_oth = lax.dot_general(
-            q, other_k[theirs, 0], contract_last, preferred_element_type=jnp.float32
-        )
-        s_own = jnp.where(lane < slots - parity * page_len, s_own * scale, -jnp.inf)
-        s_oth = jnp.where(lane < slots - (1 - parity) * page_len, s_oth * scale, -jnp.inf)
-        peak = jnp.maximum(
-            jnp.max(s_own, axis=1, keepdims=True), jnp.max(s_oth, axis=1, keepdims=True)
-        )
-        w_own, w_oth = jnp.exp(s_own - peak), jnp.exp(s_oth - peak)
-        total = jnp.sum(w_own, axis=1, keepdims=True) + jnp.sum(w_oth, axis=1, keepdims=True)
-        o = lax.dot_general(
-            w_own.astype(jnp.bfloat16), own_v[mine, 0], contract, preferred_element_type=jnp.float32
-        ) + lax.dot_general(
-            w_oth.astype(jnp.bfloat16),
-            other_v[theirs, 0],
-            contract,
+        page = table[parity, s]
+        scores = lax.dot_general(
+            qs[s].astype(jnp.bfloat16),
+            keys[page, 0],
+            (((1,), (1,)), ((), ())),
             preferred_element_type=jnp.float32,
         )
-        acc[s] = o / total
+        scores = jnp.where(lane < live[s] - parity * page_len, scores * scale, -jnp.inf)
+        peak = jnp.maximum(jnp.max(scores, axis=1, keepdims=True), -1e30)
+        weights = jnp.exp(scores - peak)
+        total = jnp.sum(weights, axis=1, keepdims=True)
+        o = lax.dot_general(
+            weights.astype(jnp.bfloat16),
+            values[page, 0],
+            (((1,), (0,)), ((), ())),
+            preferred_element_type=jnp.float32,
+        )
+        peak = jnp.broadcast_to(peak, o.shape)
+        total = jnp.broadcast_to(total, o.shape)
+        for part, to in ((slice(0, heads), mine), (slice(heads, both), theirs)):
+            to[0, s], to[1, s], to[2, s] = o[part], peak[part], total[part]
 
     def block(i, carry):
         for u in range(4):
@@ -122,8 +119,17 @@
         return carry
 
     lax.fori_loop(0, sessions // 4, block, 0)
+
+
+def combine_kernel(mine, theirs, out):
+    heads, head_dim = mine.shape[2:]
     for h in range(heads):
-        out[:, h * head_dim : (h + 1) * head_dim] = acc[:, h, :].astype(jnp.bfloat16)
+        o1, m1, l1 = (mine[i, :, h, :] for i in range(3))
+        o2, m2, l2 = (theirs[i, :, h, :] for i in range(3))
+        peak = jnp.maximum(m1, m2)
+        w1, w2 = jnp.exp(m1 - peak), jnp.exp(m2 - peak)
+        o = (o1 * w1 + o2 * w2) / (l1 * w1 + l2 * w2)
+        out[:, h * head_dim : (h + 1) * head_dim] = o.astype(jnp.bfloat16)
 
 
 def unpack_kernel(order, received, moved_k, moved_v, sem):
@@ -172,27 +178,32 @@
         axis_index_groups=groups,
         tiled=True,
     )
-    other_keys, other_values = partner((cache_keys, cache_values), "tensor", 0)
-    attention, order = pl.pallas_call(
-        attention_kernel,
-        out_shape=(
-            jax.ShapeDtypeStruct(queries.shape, jnp.bfloat16),
-            jax.ShapeDtypeStruct((replicas,), jnp.int32),
-        ),
-        in_specs=[SMEM, SMEM, SMEM, SMEM, VMEM, VMEM, VMEM, VMEM, VMEM],
-        out_specs=(VMEM, SMEM),
-        scratch_shapes=[
-            pltpu.VMEM((sessions, heads, head_dim), jnp.float32),
-            pltpu.VMEM((sessions, heads, head_dim), jnp.float32),
-        ],
+    part = jax.ShapeDtypeStruct((3, sessions, heads, head_dim), jnp.float32)
+    mine, theirs, order = pl.pallas_call(
+        partial_kernel,
+        out_shape=(part, part, jax.ShapeDtypeStruct((replicas,), jnp.int32)),
+        in_specs=[SMEM, SMEM, SMEM, SMEM, VMEM, VMEM, VMEM, VMEM],
+        out_specs=(VMEM, VMEM, SMEM),
+        scratch_shapes=[pltpu.VMEM((sessions, 2 * heads, head_dim), jnp.float32)],
         compiler_params=pltpu.CompilerParams(vmem_limit_bytes=16 * 1024 * 1024),
         cost_estimate=pl.CostEstimate(
             flops=4 * sessions * heads * row * head_dim,
-            bytes_accessed=8 * pool * page_len * head_dim,
+            bytes_accessed=4 * pool * page_len * head_dim,
             transcendentals=sessions * heads * row,
         ),
-        name="attention",
-    )(table, live_slots, moves, seat, queries, cache_keys, cache_values, other_keys, other_values)
+        name="partial",
+    )(
+        table, live_slots, moves, seat, queries, partner(queries, "tensor", 0),
+        cache_keys, cache_values,
+    )
+    attention = pl.pallas_call(
+        combine_kernel,
+        out_shape=jax.ShapeDtypeStruct(queries.shape, jnp.bfloat16),
+        in_specs=[VMEM, VMEM],
+        out_specs=VMEM,
+        compiler_params=pltpu.CompilerParams(vmem_limit_bytes=16 * 1024 * 1024),
+        name="combine",
+    )(mine, partner(theirs, "tensor", 0))
     moved = jax.ShapeDtypeStruct((replicas - 1, 1, 1, page_len, head_dim), jnp.bfloat16)
     moved_keys, moved_values = pl.pallas_call(
         unpack_kernel,

time: 66.4 us -> 66.4 us (level)
    all_to_all x1, waiting for transfers between devices: 23.5 us -> 24.4 us  [body(): lax.all_to_all(packed, ('replica', 'tensor'), split_axis=0, concat_axis=0...]
    ppermute x2, waiting for transfers between devices: 2.84 us -> 1.9 us  [partner(): lax.ppermute(x, axis, [(i, i ^ 1 << bit) for i in range(lax.axis_size(axi...]
    pallas_call x1 -> x2, Pallas kernels: 14.4 us -> 14 us  [the longest x1 13.1 us: body(): pl.pallas_call(partial_kernel, out_shape=(part, part, jax.ShapeDtypeStruc...]
  transfers between devices with their start and end apart: 3 -> 3, of which waited for: 3 -> 3; matrix products, arithmetic and copies ran while one was open for 0% -> 0% of each run, Pallas kernels for 22% -> 21%
where the time goes in v4:
time: 66.4 us; the launch traced here: 65.7 us
  waiting for transfers between devices  26.3 us (40%)
  starting transfers between devices  19 us (29%)
  Pallas kernels  18.3 us (28%)
  local copies, waits for them, and re-layouts  1.26 us (2%)
  between operations  0.75 us (1%)
    all_to_all x1, waiting for transfers between devices, body(): lax.all_to_all(packed, ('replica', 'tensor'), split_axis=0, concat_axis=0...  24.4 us
    all_to_all x1, starting transfers between devices, body(): lax.all_to_all(packed, ('replica', 'tensor'), split_axis=0, concat_axis=0...  13.3 us
    pallas_call x1, Pallas kernels, body(): pl.pallas_call(partial_kernel, out_shape=(part, part, jax.ShapeDtypeStruc...  13.1 us
    ppermute x2, starting transfers between devices, partner(): lax.ppermute(x, axis, [(i, i ^ 1 << bit) for i in range(lax.axis_size(axi...  5.67 us
    pallas_call x1, Pallas kernels, body(): pl.pallas_call(pack_kernel, out_shape=jax.ShapeDtypeStruct((replicas, row...  2.47 us
    ppermute x2, waiting for transfers between devices, partner(): lax.ppermute(x, axis, [(i, i ^ 1 << bit) for i in range(lax.axis_size(axi...  1.9 us
    pallas_call x1, Pallas kernels, body(): pl.pallas_call(unpack_kernel, out_shape=(moved, moved), in_specs=[SMEM, A...  1.82 us
  transfers between devices with their start and end apart: 3, of which 3 were waited for; matrix products, arithmetic and copies ran while one was open for 0% of the time, Pallas kernels for 21%

profile of v4, /device:TPU:56, one launch (start us, length us, event | category | flops | bytes accessed | tf_op | source)
XLA Modules:
  0.0 65.7 jit_solution(7909464708877118848)
XLA Ops:
  0.6 2.5 %pack.1 = bf16[32,256,128]{2,1,0:T(8,128)(2,1)} custom-call(s32[2,32]{1,0:T(2,128)} %bitcast.4, s32[2,256]{1,0:T(2,128)} %bitcast.2, s32[2,32]{1,0:T(2,128)} %constant.2.clone.seat.seat_hbm, bf16[32,1,128,128]{3,2,1,0:T(8,128)(2,1)} %keys.3, bf16[32,1,128,128]{3,2,1,0:T(8,128)(2,1)} %values.3), custom_call_target="tpu_custom_call" | custom-call | tf_op jit(solution)/shard_map/pack/pallas_call | solution.py:157
  3.1 0.0 copy-start.2
  3.1 0.0 copy-start
  3.1 0.0 copy-start.3
  3.1 0.0 copy-start.4
  3.2 0.0 copy-start.5
  3.2 0.0 copy-start.6
  3.2 13.3 %all-to-all-start = ((bf16[32,256,128]{2,1,0:T(8,128)(2,1)}), bf16[32,256,128]{2,1,0:T(8,128)(2,1)S(1)}, u32[]{:S(2)}, u32[]{:S(2)}) async-start(bf16[32,256,128]{2,1,0:T(8,128)(2,1)} %pack.1), calls=%async_computation | async-start | bytes 4194304 | tf_op jit(solution)/shard_map/all_to_all | solution.py:173
  16.5 0.0 copy-done.2
  16.5 3.4 %collective-permute-start = (bf16[32,512]{1,0:T(8,128)(2,1)S(1)}, bf16[32,512]{1,0:T(8,128)(2,1)S(1)}, u32[]{:S(2)}, u32[]{:S(2)}) collective-permute-start(bf16[32,512]{1,0:T(8,128)(2,1)S(1)} %copy-done.2), channel_id=1, source_target_pairs={{0,1},{1,0},{2,3},{3,2},{4,5},{5,4},{6,7},{7,6},{8,9},{9,8},{10,11... | collective-permute-start | bytes 98312 | tf_op jit(solution)/shard_map/ppermute | solution.py:21
  19.9 0.8 %collective-permute-done.other_queries = bf16[32,512]{1,0:T(8,128)(2,1)S(1)} collective-permute-done((bf16[32,512]{1,0:T(8,128)(2,1)S(1)}, bf16[32,512]{1,0:T(8,128)(2,1)S(1)}, u32[]{:S(2)}, u32[]{:S(2)}) %collective-permute-start) | collective-permute-done | bytes 32800 | tf_op jit(solution)/shard_map/ppermute | solution.py:21
  20.7 0.0 copy-done
  20.7 0.0 copy-done.3
  20.8 0.0 copy-done.4
  20.8 0.0 copy-done.5
  20.8 0.0 copy-done.6
  20.8 0.0 copy-start.1
  20.8 1.2 %copy-done.1 = bf16[32,1,128,128]{3,2,1,0:T(8,128)(2,1)S(1)} copy-done((bf16[32,1,128,128]{3,2,1,0:T(8,128)(2,1)S(1)}, bf16[32,1,128,128]{3,2,1,0:T(8,128)(2,1)}, u32[]{:S(2)}) %copy-start.1) | copy-done | bytes 1048600
  22.0 13.1 %partial.1 = (f32[3,32,4,128]{3,2,1,0:T(4,128)S(1)}, f32[3,32,4,128]{3,2,1,0:T(4,128)S(1)}, s32[32]{0:T(128)S(1)}) custom-call(s32[2,32]{1,0:T(2,128)S(1)} %bitcast.5, s32[32]{0:T(128)S(1)} %copy-done.6, s32[2,256]{1,0:T(2,128)S(1)} %bitcast.3, s32[2,32]{1,0:T(2,128)S(1)} %copy-done.5, bf16[32,512]{1,0:T(8,128)(2,1)S(1)} %copy-done.2, ...), custom_call_target="tpu_custom_call" | custom-call | flops 16777216 | bytes 2097152 | tf_op jit(solution)/shard_map/partial/pallas_call | solution.py:182
  35.1 2.3 %collective-permute-start.1 = (f32[3,32,4,128]{3,2,1,0:T(4,128)S(1)}, f32[3,32,4,128]{3,2,1,0:T(4,128)S(1)}, u32[]{:S(2)}, u32[]{:S(2)}) collective-permute-start(f32[3,32,4,128]{3,2,1,0:T(4,128)S(1)} %get-tuple-element.9), channel_id=1, source_target_pairs={{0,1},{1,0},{2,3},{3,2},{4,5},{5,4},{6,7},{7,6},{8,9},{9,8},{10,11... | collective-permute-start | bytes 589832 | tf_op jit(solution)/shard_map/ppermute | solution.py:21
  37.4 1.1 %collective-permute-done.1.theirs = f32[3,32,4,128]{3,2,1,0:T(4,128)S(1)} collective-permute-done((f32[3,32,4,128]{3,2,1,0:T(4,128)S(1)}, f32[3,32,4,128]{3,2,1,0:T(4,128)S(1)}, u32[]{:S(2)}, u32[]{:S(2)}) %collective-permute-start.1) | collective-permute-done | bytes 196640 | tf_op jit(solution)/shard_map/ppermute | solution.py:21
  38.4 0.9 %combine.1 = bf16[32,512]{1,0:T(8,128)(2,1)} custom-call(f32[3,32,4,128]{3,2,1,0:T(4,128)S(1)} %get-tuple-element.8.mine, f32[3,32,4,128]{3,2,1,0:T(4,128)S(1)} %collective-permute-done.1.theirs), custom_call_target="tpu_custom_call" | custom-call | tf_op jit(solution)/shard_map/combine/pallas_call | solution.py:199
  39.4 24.4 %all-to-all-done.received = bf16[32,256,128]{2,1,0:T(8,128)(2,1)S(1)} async-done(((bf16[32,256,128]{2,1,0:T(8,128)(2,1)}), bf16[32,256,128]{2,1,0:T(8,128)(2,1)S(1)}, u32[]{:S(2)}, u32[]{:S(2)}) %all-to-all-start) | async-done | bytes 2097184 | tf_op jit(solution)/shard_map/all_to_all | solution.py:173
  63.8 1.8 %unpack.1 = (bf16[31,1,1,128,128]{4,3,2,1,0:T(8,128)(2,1)}, bf16[31,1,1,128,128]{4,3,2,1,0:T(8,128)(2,1)}) custom-call(s32[32]{0:T(128)S(1)} %get-tuple-element.10.order, bf16[32,256,128]{2,1,0:T(8,128)(2,1)S(1)} %all-to-all-done.received), custom_call_target="tpu_custom_call" | custom-call | tf_op jit(solution)/shard_map/unpack/pallas_call | solution.py:208
Async XLA Ops:
  3.1 13.4 %copy-start.2 = (bf16[32,512]{1,0:T(8,128)(2,1)S(1)}, bf16[32,512]{1,0:T(8,128)(2,1)}, u32[]{:S(2)}) copy-start(bf16[32,512]{1,0:T(8,128)(2,1)} %queries.1) | copy-start | bytes 98308
  3.1 17.6 %copy-start = (bf16[32,1,128,128]{3,2,1,0:T(8,128)(2,1)S(1)}, bf16[32,1,128,128]{3,2,1,0:T(8,128)(2,1)}, u32[]{:S(2)}) copy-start(bf16[32,1,128,128]{3,2,1,0:T(8,128)(2,1)} %keys.3) | copy-start | bytes 3145732
  3.1 17.6 %copy-start.3 = (s32[256,2]{0,1:T(2,128)S(1)}, s32[256,2]{0,1:T(2,128)}, u32[]{:S(2)}) copy-start(s32[256,2]{0,1:T(2,128)} %param.12) | copy-start | bytes 6148
  3.1 17.6 %copy-start.4 = (s32[32,2]{0,1:T(2,128)S(1)}, s32[32,2]{0,1:T(2,128)}, u32[]{:S(2)}) copy-start(s32[32,2]{0,1:T(2,128)} %param.10) | copy-start | bytes 772
  3.2 17.6 %copy-start.5 = (s32[2,32]{1,0:T(2,128)S(1)}, s32[2,32]{1,0:T(2,128)}, u32[]{:S(2)}) copy-start(s32[2,32]{1,0:T(2,128)} %constant.2.clone.seat.seat_hbm) | copy-start | bytes 772
  3.2 17.6 %copy-start.6 = (s32[32]{0:T(128)S(1)}, s32[32]{0:T(128)}, u32[]{:S(2)}) copy-start(s32[32]{0:T(128)} %live.1) | copy-start | bytes 388
  3.2 60.7 %all-to-all-start = ((bf16[32,256,128]{2,1,0:T(8,128)(2,1)}), bf16[32,256,128]{2,1,0:T(8,128)(2,1)S(1)}, u32[]{:S(2)}, u32[]{:S(2)}) async-start(bf16[32,256,128]{2,1,0:T(8,128)(2,1)} %pack.1), calls=%async_computation | async-start | bytes 4194304 | tf_op jit(solution)/shard_map/all_to_all | solution.py:173
  16.5 4.3 %collective-permute-start = (bf16[32,512]{1,0:T(8,128)(2,1)S(1)}, bf16[32,512]{1,0:T(8,128)(2,1)S(1)}, u32[]{:S(2)}, u32[]{:S(2)}) collective-permute-start(bf16[32,512]{1,0:T(8,128)(2,1)S(1)} %copy-done.2), channel_id=1, source_target_pairs={{0,1},{1,0},{2,3},{3,2},{4,5},{5,4},{6,7},{7,6},{8,9},{9,8},{10,11... | collective-permute-start | bytes 98312 | tf_op jit(solution)/shard_map/ppermute | solution.py:21
  20.8 1.2 %copy-start.1 = (bf16[32,1,128,128]{3,2,1,0:T(8,128)(2,1)S(1)}, bf16[32,1,128,128]{3,2,1,0:T(8,128)(2,1)}, u32[]{:S(2)}) copy-start(bf16[32,1,128,128]{3,2,1,0:T(8,128)(2,1)} %values.3) | copy-start | bytes 3145732
  35.1 3.3 %collective-permute-start.1 = (f32[3,32,4,128]{3,2,1,0:T(4,128)S(1)}, f32[3,32,4,128]{3,2,1,0:T(4,128)S(1)}, u32[]{:S(2)}, u32[]{:S(2)}) collective-permute-start(f32[3,32,4,128]{3,2,1,0:T(4,128)S(1)} %get-tuple-element.9), channel_id=1, source_target_pairs={{0,1},{1,0},{2,3},{3,2},{4,5},{5,4},{6,7},{7,6},{8,9},{9,8},{10,11... | collective-permute-start | bytes 589832 | tf_op jit(solution)/shard_map/ppermute | solution.py:21

commit v5 on v3

--- a/solution.py
+++ b/solution.py
@@ -9,8 +9,14 @@
 
 OUT_ROWS = 8
 SEATS = (
-    0, 21, 10, 15, 20, 25, 30, 3, 8, 13, 18, 23, 28, 1, 6, 11,
-    16, 5, 26, 31, 4, 9, 14, 19, 24, 29, 2, 7, 12, 17, 22, 27,
+    (
+        0, 21, 10, 15, 20, 25, 30, 3, 8, 13, 18, 23, 28, 1, 6, 11,
+        16, 5, 26, 31, 4, 9, 14, 19, 24, 29, 2, 7, 12, 17, 22, 27,
+    ),
+    (
+        27, 22, 17, 12, 7, 2, 29, 24, 19, 14, 9, 4, 31, 26, 5, 16,
+        11, 6, 1, 28, 23, 18, 13, 8, 3, 30, 25, 20, 15, 10, 21, 0,
+    ),
 )
 ANY = pl.BlockSpec(memory_space=pl.ANY)
 SMEM = pl.BlockSpec(memory_space=pltpu.SMEM)
@@ -143,10 +149,9 @@
     sessions = queries.shape[0]
     heads = queries.shape[1] // head_dim
     table, moves = page_table.T, migrations.T
-    orders = (SEATS, SEATS[::-1])
-    seat = jnp.asarray([[o.index(r) for r in range(replicas)] for o in orders], jnp.int32)
+    seat = jnp.asarray([[o.index(r) for r in range(replicas)] for o in SEATS], jnp.int32)
     planes = lax.axis_size("tensor")
-    groups = [[r * planes + t for r in orders[t % 2]] for t in range(planes)]
+    groups = [[r * planes + t for r in SEATS[t % 2]] for t in range(planes)]
     row = 2 * page_len
     packed = pl.pallas_call(
         pack_kernel,

time: 66.4 us -> 66.4 us (level)
  no operation moved by 1% of the time
where the time goes in v5:
time: 66.4 us; the launch traced here: 65.7 us
  waiting for transfers between devices  26.4 us (40%)
  Pallas kernels  18.7 us (28%)
  starting transfers between devices  18.6 us (28%)
  local copies, waits for them, and re-layouts  1.26 us (2%)
  between operations  0.75 us (1%)
    all_to_all x1, waiting for transfers between devices, body(): lax.all_to_all(packed, ('replica', 'tensor'), split_axis=0, concat_axis=0...  23.5 us
    pallas_call x1, Pallas kernels, body(): pl.pallas_call(attention_kernel, out_shape=(jax.ShapeDtypeStruct(queries....  14.4 us
    all_to_all x1, starting transfers between devices, body(): lax.all_to_all(packed, ('replica', 'tensor'), split_axis=0, concat_axis=0...  13.3 us
    ppermute x2, starting transfers between devices, partner(): lax.ppermute(x, axis, [(i, i ^ 1 << bit) for i in range(lax.axis_size(axi...  5.33 us
    ppermute x2, waiting for transfers between devices, partner(): lax.ppermute(x, axis, [(i, i ^ 1 << bit) for i in range(lax.axis_size(axi...  2.84 us
    pallas_call x1, Pallas kernels, body(): pl.pallas_call(pack_kernel, out_shape=jax.ShapeDtypeStruct((replicas, row...  2.46 us
    pallas_call x1, Pallas kernels, body(): pl.pallas_call(unpack_kernel, out_shape=(moved, moved), in_specs=[SMEM, A...  1.82 us
  transfers between devices with their start and end apart: 3, of which 3 were waited for; matrix products, arithmetic and copies ran while one was open for 0% of the time, Pallas kernels for 22%

profile of v5, /device:TPU:56, one launch (start us, length us, event | category | flops | bytes accessed | tf_op | source)
XLA Modules:
  0.0 65.7 jit_solution(2947210469060961010)
XLA Ops:
  0.6 2.5 %pack.1 = bf16[32,256,128]{2,1,0:T(8,128)(2,1)} custom-call(s32[2,32]{1,0:T(2,128)} %bitcast.4, s32[2,256]{1,0:T(2,128)} %bitcast.2, s32[2,32]{1,0:T(2,128)} %constant.2.clone.seat.seat_hbm, bf16[32,1,128,128]{3,2,1,0:T(8,128)(2,1)} %keys.1, bf16[32,1,128,128]{3,2,1,0:T(8,128)(2,1)} %values.1), custom_call_target="tpu_custom_call" | custom-call | tf_op jit(solution)/shard_map/pack/pallas_call | solution.py:156
  3.1 0.0 copy-start
  3.1 0.0 copy-start.2
  3.1 0.0 copy-start.3
  3.1 0.0 copy-start.4
  3.1 0.0 copy-start.5
  3.2 0.0 copy-start.6
  3.2 13.3 %all-to-all-start = ((bf16[32,256,128]{2,1,0:T(8,128)(2,1)}), bf16[32,256,128]{2,1,0:T(8,128)(2,1)S(1)}, u32[]{:S(2)}, u32[]{:S(2)}) async-start(bf16[32,256,128]{2,1,0:T(8,128)(2,1)} %pack.1), calls=%async_computation | async-start | bytes 4194304 | tf_op jit(solution)/shard_map/all_to_all | solution.py:172
  16.5 0.0 copy-done
  16.5 3.4 %collective-permute-start = (bf16[32,1,128,128]{3,2,1,0:T(8,128)(2,1)S(1)}, bf16[32,1,128,128]{3,2,1,0:T(8,128)(2,1)S(1)}, u32[]{:S(2)}, u32[]{:S(2)}) collective-permute-start(bf16[32,1,128,128]{3,2,1,0:T(8,128)(2,1)S(1)} %copy-done), channel_id=1, source_target_pairs={{0,1},{1,0},{2,3},{3,2},{4,5},{5,4},{6,7},{7,6},{8,9},{9,8},{10,11... | collective-permute-start | bytes 3145736 | tf_op jit(solution)/shard_map/ppermute | solution.py:27
  19.9 1.9 %collective-permute-start.1 = (bf16[32,1,128,128]{3,2,1,0:T(8,128)(2,1)}, bf16[32,1,128,128]{3,2,1,0:T(8,128)(2,1)S(1)}, u32[]{:S(2)}, u32[]{:S(2)}) collective-permute-start(bf16[32,1,128,128]{3,2,1,0:T(8,128)(2,1)} %values.1), channel_id=1, source_target_pairs={{0,1},{1,0},{2,3},{3,2},{4,5},{5,4},{6,7},{7,6},{8,9},{9,8},{10,11... | collective-permute-start | bytes 3145736 | tf_op jit(solution)/shard_map/ppermute | solution.py:27
  21.8 0.3 collective-permute-done.other_k
  22.2 2.5 %collective-permute-done.1.other_v = bf16[32,1,128,128]{3,2,1,0:T(8,128)(2,1)S(1)} collective-permute-done((bf16[32,1,128,128]{3,2,1,0:T(8,128)(2,1)}, bf16[32,1,128,128]{3,2,1,0:T(8,128)(2,1)S(1)}, u32[]{:S(2)}, u32[]{:S(2)}) %collective-permute-start.1) | collective-permute-done | bytes 1048608 | tf_op jit(solution)/shard_map/ppermute | solution.py:27
  24.7 0.0 copy-done.2
  24.7 0.0 copy-done.3
  24.7 0.0 copy-done.4
  24.7 0.0 copy-done.5
  24.7 0.0 copy-done.6
  24.7 0.0 copy-start.1
  24.7 1.2 %copy-done.1 = bf16[32,1,128,128]{3,2,1,0:T(8,128)(2,1)S(1)} copy-done((bf16[32,1,128,128]{3,2,1,0:T(8,128)(2,1)S(1)}, bf16[32,1,128,128]{3,2,1,0:T(8,128)(2,1)}, u32[]{:S(2)}) %copy-start.1) | copy-done | bytes 1048600
  25.9 14.4 %attention.1 = (bf16[32,512]{1,0:T(8,128)(2,1)}, s32[32]{0:T(128)S(1)}) custom-call(s32[2,32]{1,0:T(2,128)S(1)} %bitcast.5, s32[32]{0:T(128)S(1)} %copy-done.6, s32[2,256]{1,0:T(2,128)S(1)} %bitcast.3, s32[2,32]{1,0:T(2,128)S(1)} %copy-done.5, bf16[32,512]{1,0:T(8,128)(2,1)S(1)} %copy-done.2, bf16[32,1,128,128]{3,2,1,0:T(8,128)(2,1)S(1)} %copy-done, ...), custom_call_target="tpu_custom_call" | custom-call | flops 16777216 | bytes 4194304 | tf_op jit(solution)/shard_map/attention/pallas_call | solution.py:181
  40.3 23.5 %all-to-all-done.received = bf16[32,256,128]{2,1,0:T(8,128)(2,1)S(1)} async-done(((bf16[32,256,128]{2,1,0:T(8,128)(2,1)}), bf16[32,256,128]{2,1,0:T(8,128)(2,1)S(1)}, u32[]{:S(2)}, u32[]{:S(2)}) %all-to-all-start) | async-done | bytes 2097184 | tf_op jit(solution)/shard_map/all_to_all | solution.py:172
  63.8 1.8 %unpack.1 = (bf16[31,1,1,128,128]{4,3,2,1,0:T(8,128)(2,1)}, bf16[31,1,1,128,128]{4,3,2,1,0:T(8,128)(2,1)}) custom-call(s32[32]{0:T(128)S(1)} %get-tuple-element.8.order, bf16[32,256,128]{2,1,0:T(8,128)(2,1)S(1)} %all-to-all-done.received), custom_call_target="tpu_custom_call" | custom-call | tf_op jit(solution)/shard_map/unpack/pallas_call | solution.py:202
Async XLA Ops:
  3.1 13.4 %copy-start = (bf16[32,1,128,128]{3,2,1,0:T(8,128)(2,1)S(1)}, bf16[32,1,128,128]{3,2,1,0:T(8,128)(2,1)}, u32[]{:S(2)}) copy-start(bf16[32,1,128,128]{3,2,1,0:T(8,128)(2,1)} %keys.1) | copy-start | bytes 3145732
  3.1 21.6 %copy-start.2 = (bf16[32,512]{1,0:T(8,128)(2,1)S(1)}, bf16[32,512]{1,0:T(8,128)(2,1)}, u32[]{:S(2)}) copy-start(bf16[32,512]{1,0:T(8,128)(2,1)} %queries.1) | copy-start | bytes 98308
  3.1 21.6 %copy-start.3 = (s32[256,2]{0,1:T(2,128)S(1)}, s32[256,2]{0,1:T(2,128)}, u32[]{:S(2)}) copy-start(s32[256,2]{0,1:T(2,128)} %param.12) | copy-start | bytes 6148
  3.1 21.6 %copy-start.4 = (s32[32,2]{0,1:T(2,128)S(1)}, s32[32,2]{0,1:T(2,128)}, u32[]{:S(2)}) copy-start(s32[32,2]{0,1:T(2,128)} %param.10) | copy-start | bytes 772
  3.1 21.5 %copy-start.5 = (s32[2,32]{1,0:T(2,128)S(1)}, s32[2,32]{1,0:T(2,128)}, u32[]{:S(2)}) copy-start(s32[2,32]{1,0:T(2,128)} %constant.2.clone.seat.seat_hbm) | copy-start | bytes 772
  3.2 21.5 %copy-start.6 = (s32[32]{0:T(128)S(1)}, s32[32]{0:T(128)}, u32[]{:S(2)}) copy-start(s32[32]{0:T(128)} %live.1) | copy-start | bytes 388
  3.2 60.7 %all-to-all-start = ((bf16[32,256,128]{2,1,0:T(8,128)(2,1)}), bf16[32,256,128]{2,1,0:T(8,128)(2,1)S(1)}, u32[]{:S(2)}, u32[]{:S(2)}) async-start(bf16[32,256,128]{2,1,0:T(8,128)(2,1)} %pack.1), calls=%async_computation | async-start | bytes 4194304 | tf_op jit(solution)/shard_map/all_to_all | solution.py:172
  16.5 5.7 %collective-permute-start = (bf16[32,1,128,128]{3,2,1,0:T(8,128)(2,1)S(1)}, bf16[32,1,128,128]{3,2,1,0:T(8,128)(2,1)S(1)}, u32[]{:S(2)}, u32[]{:S(2)}) collective-permute-start(bf16[32,1,128,128]{3,2,1,0:T(8,128)(2,1)S(1)} %copy-done), channel_id=1, source_target_pairs={{0,1},{1,0},{2,3},{3,2},{4,5},{5,4},{6,7},{7,6},{8,9},{9,8},{10,11... | collective-permute-start | bytes 3145736 | tf_op jit(solution)/shard_map/ppermute | solution.py:27
  19.9 4.8 %collective-permute-start.1 = (bf16[32,1,128,128]{3,2,1,0:T(8,128)(2,1)}, bf16[32,1,128,128]{3,2,1,0:T(8,128)(2,1)S(1)}, u32[]{:S(2)}, u32[]{:S(2)}) collective-permute-start(bf16[32,1,128,128]{3,2,1,0:T(8,128)(2,1)} %values.1), channel_id=1, source_target_pairs={{0,1},{1,0},{2,3},{3,2},{4,5},{5,4},{6,7},{7,6},{8,9},{9,8},{10,11... | collective-permute-start | bytes 3145736 | tf_op jit(solution)/shard_map/ppermute | solution.py:27
  24.7 1.2 %copy-start.1 = (bf16[32,1,128,128]{3,2,1,0:T(8,128)(2,1)S(1)}, bf16[32,1,128,128]{3,2,1,0:T(8,128)(2,1)}, u32[]{:S(2)}) copy-start(bf16[32,1,128,128]{3,2,1,0:T(8,128)(2,1)} %values.1) | copy-start | bytes 3145732
